TPU v7x, 32 devices: a whole 2x2x4 slice. The times are simulated.
32 devices in a mesh: pb: 16 (over z, x, core), ka: 2 (over y).
Axes of the slice: x: 2, y: 2, z: 4, core: 2. Of those that a mesh axis runs over, the one named last changes fastest.
Arguments:
- queries: bfloat16 [4096, 1024], P('pb'), may hold values from -40 to 40
- keys: bfloat16 [4096, 128], P(('ka', 'pb')), may hold values from -20 to 20
- values: bfloat16 [4096, 128], P(('ka', 'pb')), may hold values from -12 to 12
- dout: bfloat16 [4096, 1024], P('pb'), may hold values from -6 to 6
- block_mask: int32 [32, 32], P('pb', 'ka'), may hold values from 0 to 1, as said below
Outputs:
- attended: bfloat16 [4096, 1024], P('pb', 'ka')
- query_grad: float32 [4096, 1024], P('pb', 'ka')
- key_grad: float32 [4096, 128], P(('ka', 'pb'))
- value_grad: float32 [4096, 128], P(('ka', 'pb'))
Inputs may be any that keep to these rules, and one draw needn't show every extreme that they name: block_mask[i, j] = 1 lets the 128 queries of block i see the 128 keys of block j. Rows 2 * i and 2 * i + 1 are equal; in both of them the entries of columns 2 * i and 2 * i + 1 are 1, and every aligned run of 16 columns holds at least one 1.
All inputs are finite; a program needn't handle non-finite values.
Results may differ from a plain program's by a relative error of at most 0.017.
Values may be sent and summed in bfloat16 or wider, within the bound.
A program may use at most 64 MiB of HBM per device.

v0:
```python
import math

import jax
import jax.numpy as jnp
from jax import lax
from jax.sharding import PartitionSpec as P

BLOCK = 128


def merged_2(part, axis, combine):
    gathered = jax.tree.map(lambda a: lax.all_gather(a, axis), part)

    def take(source):
        return jax.tree.map(lambda a: lax.dynamic_index_in_dim(a, source, 0, False), gathered)

    return lax.fori_loop(
        1, lax.axis_size(axis), lambda source, state: combine(state, take(source)), take(0)
    )


def tile_live(mask_tile):
    expanded = jnp.repeat(jnp.repeat(mask_tile, BLOCK, axis=0), BLOCK, axis=1)
    return (expanded > 0)[None]


def tile_scores(query_heads, key_tile, score_scale):
    return (
        jnp.einsum("qhd,kd->hqk", query_heads, key_tile, preferred_element_type=jnp.float32)
        * score_scale
    )


def guarded(compute, carry):
    result = compute(carry)
    return result


def fold_parts(part_one, part_two):
    lse_one, out_one = part_one
    lse_two, out_two = part_two
    row_peak = jnp.maximum(lse_one, lse_two)
    joint_lse = row_peak + jnp.log(jnp.exp(lse_one - row_peak) + jnp.exp(lse_two - row_peak))
    mixed_out = (
        out_one * jnp.exp(lse_one - joint_lse)[:, :, None]
        + out_two * jnp.exp(lse_two - joint_lse)[:, :, None]
    )
    return (joint_lse, mixed_out)


def per_device(queries, keys, values, dout, block_mask):
    query_rows, row_width = queries.shape
    head_width = keys.shape[1]
    head_count = row_width // head_width
    heads_own = head_count // lax.axis_size("ka")
    score_scale = 1.0 / math.sqrt(head_width)
    query_heads = queries.reshape(query_rows, head_count, head_width)
    dout_heads = dout.reshape(query_rows, head_count, head_width)
    key_panel, value_panel = (
        lax.all_gather(keys, "pb", axis=0, tiled=True),
        lax.all_gather(values, "pb", axis=0, tiled=True),
    )
    tile_width = BLOCK
    tile_count = key_panel.shape[0] // tile_width
    key_tiles = key_panel.reshape(tile_count, tile_width, head_width)
    value_tiles = value_panel.reshape(tile_count, tile_width, head_width)
    mask_tiles = block_mask.reshape(block_mask.shape[0], tile_count, 1).transpose(1, 0, 2)

    def peak_step(row_max, inputs):
        key_tile, mask_tile = inputs

        def compute(current):
            masked = jnp.where(
                tile_live(mask_tile), tile_scores(query_heads, key_tile, score_scale), -jnp.inf
            )
            return jnp.maximum(current, jnp.max(masked, axis=2))

        return (guarded(compute, row_max), None)

    max_start = jnp.full((head_count, query_rows), -jnp.inf, jnp.float32)
    panel_max, _ = lax.scan(peak_step, max_start, (key_tiles, mask_tiles))

    def total_step(carry, inputs):
        key_tile, value_tile, mask_tile = inputs

        def compute(running):
            running_total, running_acc = running
            scores = tile_scores(query_heads, key_tile, score_scale)
            weights = jnp.where(tile_live(mask_tile), jnp.exp(scores - panel_max[:, :, None]), 0.0)
            running_acc = running_acc + jnp.einsum(
                "hqk,kd->hqd",
                weights.astype(jnp.bfloat16),
                value_tile,
                preferred_element_type=jnp.float32,
            )
            return (running_total + jnp.sum(weights, axis=2), running_acc)

        return (guarded(compute, carry), None)

    zeros_total = jnp.zeros((head_count, query_rows), jnp.float32)
    zeros_acc = jnp.zeros((head_count, query_rows, head_width), jnp.float32)
    (panel_total, panel_acc), _ = lax.scan(
        total_step, (zeros_total, zeros_acc), (key_tiles, value_tiles, mask_tiles)
    )
    panel_out = lax.optimization_barrier(
        (panel_acc / panel_total[:, :, None]).astype(jnp.bfloat16)
    ).astype(jnp.float32)
    panel_lse = panel_max + jnp.log(panel_total)
    panel_index = lax.axis_index("ka")
    row_lse, merged = merged_2((panel_lse, panel_out), "ka", fold_parts)
    full_out = merged.astype(jnp.bfloat16)
    row_delta = jnp.sum(
        dout_heads.astype(jnp.float32).transpose(1, 0, 2) * full_out.astype(jnp.float32), axis=2
    )
    own_out = lax.dynamic_slice_in_dim(full_out, panel_index * heads_own, heads_own, 0)
    attended = own_out.transpose(1, 0, 2).reshape(query_rows, heads_own * head_width)

    def grad_step(carry, inputs):
        key_tile, value_tile, mask_tile = inputs

        def compute(grad_acc):
            scores = tile_scores(query_heads, key_tile, score_scale)
            probs = jnp.where(tile_live(mask_tile), jnp.exp(scores - row_lse[:, :, None]), 0.0)
            probs_low = probs.astype(jnp.bfloat16)
            value_part = jnp.einsum(
                "hqk,qhd->kd", probs_low, dout_heads, preferred_element_type=jnp.float32
            )
            dprobs = jnp.einsum(
                "qhd,kd->hqk", dout_heads, value_tile, preferred_element_type=jnp.float32
            )
            dscores = (probs * (dprobs - row_delta[:, :, None])).astype(jnp.bfloat16)
            grad_acc = grad_acc + jnp.einsum(
                "hqk,kd->qhd", dscores, key_tile, preferred_element_type=jnp.float32
            )
            key_part = (
                jnp.einsum("hqk,qhd->kd", dscores, query_heads, preferred_element_type=jnp.float32)
                * score_scale
            )
            return (grad_acc, key_part, value_part)

        grad_acc, key_part, value_part = guarded(compute, carry)
        return (grad_acc, (key_part, value_part))

    grad_start = jnp.zeros((query_rows, head_count, head_width), jnp.float32)
    grad_acc, (key_parts, value_parts) = lax.scan(
        grad_step, grad_start, (key_tiles, value_tiles, mask_tiles)
    )
    panel_dq = lax.optimization_barrier((grad_acc * score_scale).astype(jnp.bfloat16)).astype(
        jnp.float32
    )
    query_grad = lax.psum_scatter(
        panel_dq.reshape(query_rows, row_width).astype(jnp.bfloat16),
        "ka",
        scatter_dimension=1,
        tiled=True,
    ).astype(jnp.float32)
    key_grad, value_grad = (
        lax.psum_scatter(key_parts.reshape(-1, head_width), "pb", scatter_dimension=0, tiled=True),
        lax.psum_scatter(
            value_parts.reshape(-1, head_width), "pb", scatter_dimension=0, tiled=True
        ),
    )
    return (attended, query_grad, key_grad, value_grad)


def solution(mesh):
    in_specs = (
        P("pb", None),
        P(("ka", "pb"), None),
        P(("ka", "pb"), None),
        P("pb", None),
        P("pb", "ka"),
    )
    out_specs = (P("pb", "ka"), P("pb", "ka"), P(("ka", "pb"), None), P(("ka", "pb"), None))
    return jax.shard_map(
        per_device, mesh=mesh, in_specs=in_specs, out_specs=out_specs, check_vma=False
    )
```

profile of v0, /device:TPU:0, one launch (start us, length us, event | category | flops | bytes accessed | tf_op | source)
XLA Modules:
  0.0 358.9 jit_solution(14055955994575860168)
XLA Ops:
  8.0 24.8 %all_gather.21 = bf16[2048,128]{1,0:T(8,128)(2,1)S(1)} all-gather(bf16[128,128]{1,0:T(8,128)(2,1)} %param.12), channel_id=1, replica_groups=mesh['pb'=16,'ka'=2] {'pb'}, dimensions={0}, use_global_device_ids=true | all-gather | bytes 557056 | tf_op jit(solution)/shard_map/all_gather | solution.py:60
  32.8 1.2 copy.35
  34.3 7.0 %while.45 = (s32[]{:T(128)}, f32[8,256]{1,0:T(8,128)S(1)}, s32[16,2,1]{1,2,0:T(1,128)S(1)}, bf16[16,128,128]{2,1,0:T(8,128)(2,1)S(1)}, bf16[256,8,128]{2,0,1:T(8,128)(2,1)S(1)}, /*index=5*/s32[]{:T(128)}, s32[]{:T(128)}) while((s32[]{:T(128)}, f32[8,256]{1,0:T(8,128)S(1)}, s32[16,2,1]{1,2,0:T(1,128)S(1)}, ...), condition=%wide.region_2.3_spmd.clone, body=%wide.region_0.2_spmd.clone.sunk | while | flops 67897344 | bytes 590707 | solution.py:81
  41.3 18.9 %all_gather.22 = bf16[2048,128]{1,0:T(8,128)(2,1)S(1)} all-gather(bf16[128,128]{1,0:T(8,128)(2,1)S(1)} %copy-done.3), channel_id=1, replica_groups=mesh['pb'=16,'ka'=2] {'pb'}, dimensions={0}, use_global_device_ids=true | all-gather | bytes 557056 | tf_op jit(solution)/shard_map/all_gather | solution.py:61
  60.2 16.1 %while.46 = (s32[]{:T(128)}, f32[8,256]{1,0:T(8,128)S(1)}, f32[8,256,128]{2,1,0:T(8,128)S(1)}, s32[16,2,1]{1,2,0:T(1,128)S(1)}, bf16[16,128,128]{2,1,0:T(8,128)(...) while((s32[]{:T(128)}, f32[8,256]{1,0:T(8,128)S(1)}, ...), condition=%wide.region_5.6_spmd.clone, body=%wide.region_3.5_spmd.clone.sunk | while | flops 136054784 | bytes 3777424 | solution.py:102
  78.4 4.4 %all-gather.1 = f32[16,256]{1,0:T(8,128)S(1)} all-gather(f32[8,256]{1,0:T(8,128)S(1)} %log_add_fusion.1), channel_id=3, replica_groups=mesh['pb'=16,'ka'=2] {'ka'}, dimensions={0}, use_global_device_ids=true | all-gather | bytes 24576 | tf_op jit(solution)/shard_map/all_gather | solution.py:12
  82.8 26.7 %all-gather.4.cloned.1.call-done = f32[16,256,128]{2,1,0:T(8,128)} async-done(((f32[8,256,128]{2,1,0:T(8,128)}), f32[16,256,128]{2,1,0:T(8,128)}) %all-gather.4.cloned.1.call-update) | async-done | bytes 2097168 | tf_op jit(solution)/shard_map/all_gather | solution.py:12
  109.5 3.1 fusion.41
  112.6 1.6 copy.54
  114.2 2.5 copy.53
  116.7 2.3 fusion.38
  119.0 93.7 %while.47 = (s32[]{:T(128)}, f32[256,8,128]{0,2,1:T(8,128)}, f32[16,128,128]{2,1,0:T(8,128)}, f32[16,128,128]{2,1,0:T(8,128)}, bf16[16,128,128]{2,1,0:T(8,128)(2...) while((s32[]{:T(128)}, f32[256,8,128]{0,2,1:T(8,128)}, ...), condition=%wide.region_8.9_spmd.clone, body=%wide.region_7.8_spmd.clone.sunk | while | flops 337920000 | bytes 9159347 | solution.py:145
  119.1 1.1 fusion.90
  120.5 2.1 fusion.92
  124.5 1.1 fusion.90
  125.9 2.6 fusion.92
  130.4 1.1 fusion.90
  131.8 2.6 fusion.92
  136.2 1.1 fusion.90
  137.7 2.6 fusion.92
  142.1 1.1 fusion.90
  143.6 2.6 fusion.92
  148.0 1.1 fusion.90
  149.5 2.6 fusion.92
  153.9 1.1 fusion.90
  155.3 2.6 fusion.92
  159.8 1.1 fusion.90
  161.2 2.6 fusion.92
  165.7 1.1 fusion.90
  167.1 2.6 fusion.92
  171.6 1.1 fusion.90
  173.0 2.6 fusion.92
  177.4 1.1 fusion.90
  178.9 2.6 fusion.92
  183.3 1.1 fusion.90
  184.8 2.6 fusion.92
  190.7 2.6 fusion.92
  195.1 1.1 fusion.90
  196.5 2.6 fusion.92
  201.0 1.1 fusion.90
  202.4 2.6 fusion.92
  206.9 1.1 fusion.90
  208.3 2.6 fusion.92
  212.7 1.3 multiply_convert_fusion
  217.3 12.5 %reduce-scatter.4.cloned.1.call-done = bf16[256,512]{1,0:T(8,128)(2,1)} async-done(((bf16[256,1024]{1,0:T(8,128)(2,1)}), bf16[256,512]{1,0:T(8,128)(2,1)}) %reduce-scatter.4.cloned.1.call-update) | async-done | bytes 262160 | tf_op jit(solution)/shard_map/reduce_scatter | solution.py:151
  229.8 1.8 convert_element_type.36
  231.6 60.3 %reduce-scatter.6.cloned.1.call-done = f32[128,128]{1,0:T(8,128)} async-done(((f32[2048,128]{1,0:T(8,128)}), f32[128,128]{1,0:T(8,128)}) %reduce-scatter.6.cloned.1.call-update) | async-done | bytes 65552 | tf_op jit(solution)/shard_map/reduce_scatter | solution.py:158
  291.9 60.4 %reduce-scatter.8.cloned.1.call-done = f32[128,128]{1,0:T(8,128)} async-done(((f32[2048,128]{1,0:T(8,128)}), f32[128,128]{1,0:T(8,128)}) %reduce-scatter.8.cloned.1.call-update) | async-done | bytes 65552 | tf_op jit(solution)/shard_map/reduce_scatter | solution.py:159
  (259 shorter events, 64.1 us)
Async XLA Ops:
  7.2 102.4 %all-gather.4.cloned.1.call-start = ((), (), s32[]{:S(2)}) async-start(), calls=%async_computation.6 | async-start | bytes 3145728 | tf_op jit(solution)/shard_map/all_gather | solution.py:12
  34.3 7.0 %copy-start.3 = (bf16[128,128]{1,0:T(8,128)(2,1)S(1)}, bf16[128,128]{1,0:T(8,128)(2,1)}, u32[]{:S(2)}) copy-start(bf16[128,128]{1,0:T(8,128)(2,1)} %param.13) | copy-start | bytes 98308
  76.3 1.5 copy-start
  76.3 1.6 copy-start.2
  77.8 152.0 %reduce-scatter.4.cloned.1.call-start = ((), (), s32[]{:S(2)}) async-start(), calls=%async_computation.3 | async-start | bytes 786432 | tf_op jit(solution)/shard_map/reduce_scatter | solution.py:151
  214.0 2.4 copy-start.1
  215.1 76.8 %reduce-scatter.6.cloned.1.call-start = ((), (), s32[]{:S(2)}) async-start(), calls=%async_computation.4 | async-start | bytes 1114112 | tf_op jit(solution)/shard_map/reduce_scatter | solution.py:158
  215.8 136.5 %reduce-scatter.8.cloned.1.call-start = ((), (), s32[]{:S(2)}) async-start(), calls=%async_computation.5 | async-start | bytes 1114112 | tf_op jit(solution)/shard_map/reduce_scatter | solution.py:159
Sparse Core Ops, SparseCore 0:
  77.9 31.5 all-gather.3
  215.2 14.5 reduce-scatter.3
  234.4 57.4 reduce-scatter.5
  295.9 56.3 reduce-scatter.7
where the time goes:
time: 361 us; the launch traced here: 359 us
  waiting for transfers between devices  161 us (45%)
  matrix products  111 us (31%)
  blocking collectives  48.1 us (13%)
  local copies, waits for them, and re-layouts  15.4 us (4%)
  between operations  14 us (4%)
  other arithmetic  7.47 us (2%)
    reduce_scatter x1, waiting for transfers between devices, per_device(): lax.psum_scatter(value_parts.reshape(-1, head_width), 'pb', scatter_dimen...  60.4 us
    reduce_scatter x1, waiting for transfers between devices, per_device(): lax.psum_scatter(key_parts.reshape(-1, head_width), 'pb', scatter_dimensi...  60.3 us
    dot_general x16, matrix products, compute(): jnp.einsum('hqk,kd->qhd', dscores, key_tile, preferred_element_type=jnp.f...  40.5 us
    dot_general x48, matrix products, tile_scores(): jnp.einsum('qhd,kd->hqk', query_heads, key_tile, preferred_element_type=j...  29.1 us
    all_gather x1, waiting for transfers between devices, merged_2(): gathered = jax.tree.map(lambda a: lax.all_gather(a, axis), part)  26.7 us
    all_gather x1, blocking collectives, per_device(): lax.all_gather(keys, 'pb', axis=0, tiled=True)  24.8 us
    all_gather x1, blocking collectives, per_device(): lax.all_gather(values, 'pb', axis=0, tiled=True)  18.9 us
    dot_general x16, matrix products, compute(): jnp.einsum('hqk,qhd->kd', dscores, query_heads, preferred_element_type=jn...  14.5 us
  transfers between devices with their start and end apart: 4, of which 4 were waited for; matrix products, arithmetic and copies ran while one was open for 1% of the time, Pallas kernels for 0%

commit v1 on v0

v1 whole, which is shorter than its diff:
```python
import functools
import math

import jax
import jax.numpy as jnp
from jax import lax
from jax.experimental import pallas as pl
from jax.experimental.pallas import tpu as pltpu
from jax.sharding import PartitionSpec as P

BLOCK = 128
DEAD = 1e30
F32 = jnp.float32
BF16 = jnp.bfloat16


def dot_nn(a, b):
    return jnp.dot(a, b, preferred_element_type=F32)


def dot_nt(a, b):
    return lax.dot_general(a, b, (((1,), (1,)), ((), ())), preferred_element_type=F32)


def kernel(
    n_pb, n_ka,
    mask_ref, q_ref, k_ref, v_ref, do_ref,
    att_ref, qg_ref, kg_ref, vg_ref,
    kv, k_turned, q_turned, do_turned, q_scaled, do_scaled, weights, dscores,
    out_acc, dq_acc, run_max, run_total, group_max, row_lse, row_delta,
    stat_recv, out_send, out_recv, dq_send, dq_recv,
    acc, core_send, core_recv, x_send, x_recv, z_send, z_recv,
    ag_recv_sem, ag_z_sem, ag_x_sem, ag_core_sem,
    stat_send_sem, stat_recv_sem, out_send_sem, out_recv_sem, dq_send_sem, dq_recv_sem,
    core_send_sem, core_recv_sem, x_send_sem, x_recv_sem, z_send_sem, z_recv_sem,
):
    rows, width = q_ref.shape
    chunk, dim = k_ref.shape
    heads = width // dim
    own_heads = heads // n_ka
    groups = n_pb // 4
    group_keys = 4 * chunk
    group_blocks = group_keys // BLOCK
    scale = 1.0 / math.sqrt(dim)
    log_scale = scale * math.log2(math.e)

    me = lax.axis_index("pb")
    panel = lax.axis_index("ka")
    core = lax.rem(me, 2)
    x = lax.rem(me // 2, 2)
    z = me // 4
    other_core, other_x = 1 - core, 1 - x

    def at(z_index, x_index, core_index):
        return (z_index * 2 + x_index) * 2 + core_index

    core_peer, x_peer = at(z, x, other_core), at(z, other_x, core)

    def remote(src, dst, send_sem, recv_sem, device):
        return pltpu.make_async_remote_copy(
            src_ref=src, dst_ref=dst, send_sem=send_sem, recv_sem=recv_sem,
            device_id=device, device_id_type=pl.DeviceIdType.MESH,
        )

    def ring(start, step, size):
        return lax.rem(start + step, size)

    barrier = pltpu.get_barrier_semaphore()
    partners = [{"pb": core_peer}, {"pb": x_peer}]
    partners += [{"pb": at(ring(z, s, groups), x, core)} for s in range(1, groups)]
    partners += [{"ka": ring(panel, s, n_ka)} for s in range(1, n_ka)]
    for partner in partners:
        pl.semaphore_signal(barrier, inc=1, device_id=partner, device_id_type=pl.DeviceIdType.MESH)
    kv[me, 0:chunk, :] = k_ref[...]
    kv[me, chunk : 2 * chunk, :] = v_ref[...]
    pl.semaphore_wait(barrier, len(partners))

    def gather_copy(index, send_sem, device):
        return remote(kv.at[index], kv.at[index], send_sem, ag_recv_sem.at[index], {"pb": device})

    def z_copy(s):
        return gather_copy(me, ag_z_sem.at[s], at(ring(z, s, groups), x, core))

    def x_copy(k):
        return gather_copy(at(ring(z, k, groups), x, core), ag_x_sem.at[k], x_peer)

    def core_copy(k, part):
        owner_x = x if part == 0 else other_x
        index = at(ring(z, k, groups), owner_x, core)
        return gather_copy(index, ag_core_sem.at[2 * k + part], core_peer)

    def arrived(index):
        gather_copy(index, ag_x_sem.at[0], core_peer).wait_recv()

    x_copy(0).start()
    core_copy(0, 0).start()
    for s in range(1, groups):
        z_copy(s).start()

    def head_columns(head):
        return pl.ds(pl.multiple_of(head * rows, rows), rows)

    def head_at(i):
        return lax.rem((panel + 1) * own_heads + i, heads)

    for head in range(heads):
        source = pl.ds(head * dim, dim)
        target = pl.ds(head * rows, rows)
        q_turned[:, target] = q_ref[:, source].T
        do_turned[:, target] = do_ref[:, source].T
    out_acc[...] = jnp.zeros_like(out_acc)
    dq_acc[...] = jnp.zeros_like(dq_acc)
    run_max[...] = jnp.full_like(run_max, -1e38)
    run_total[...] = jnp.zeros_like(run_total)

    def stage_x(k):
        arrived(at(ring(z, k, groups), other_x, core))
        core_copy(k, 1).start()

    def stage_core(k):
        arrived(at(ring(z, k, groups), x, other_core))
        arrived(at(ring(z, k, groups), other_x, other_core))

    stage_x(0)
    stage_core(0)

    def group_rows(group, first):
        return kv[pl.ds(group * 4, 4), first : first + chunk, :].reshape(group_keys, dim)

    def forward_group(k, _):
        group = ring(z, k, groups)
        more = k < groups - 1

        @pl.when(more)
        def _():
            arrived(at(ring(z, k + 1, groups), x, core))
            x_copy(k + 1).start()
            core_copy(k + 1, 0).start()

        keys = group_rows(group, 0)
        k_turned[group] = keys.T
        values_turned = group_rows(group, chunk).T
        bias = [
            (mask_ref[0, group * group_blocks + b].astype(F32) - 1.0) * DEAD
            for b in range(group_blocks)
        ]

        def forward_head(i, _):
            cols = head_columns(head_at(i))
            scores = dot_nn(group_rows(group, 0), q_turned[:, cols])
            parts = [
                scores[b * BLOCK : (b + 1) * BLOCK] * log_scale + bias[b]
                for b in range(group_blocks)
            ]
            peak = functools.reduce(
                jnp.maximum, [jnp.max(part, axis=0, keepdims=True) for part in parts]
            )
            low = []
            total = jnp.zeros_like(peak)
            for part in parts:
                weight = jnp.exp2(part - peak)
                total = total + jnp.sum(weight, axis=0, keepdims=True)
                low.append(weight.astype(BF16))
            low = jnp.concatenate(low, axis=0)
            weights[group, :, cols] = low
            group_max[group, :, cols] = peak
            old = run_max[:, cols]
            new = jnp.maximum(old, peak)
            keep, add = jnp.exp2(old - new), jnp.exp2(peak - new)
            run_max[:, cols] = new
            run_total[:, cols] = run_total[:, cols] * keep + total * add
            out_acc[:, cols] = out_acc[:, cols] * keep + dot_nn(values_turned, low) * add
            return 0

        lax.fori_loop(0, heads // 2, forward_head, 0, unroll=2)

        @pl.when(more)
        def _():
            stage_x(k + 1)

        lax.fori_loop(heads // 2, heads, forward_head, 0, unroll=2)

        @pl.when(more)
        def _():
            stage_core(k + 1)

        return 0

    lax.fori_loop(0, groups, forward_group, 0)

    def stat_copy(head, s):
        return remote(
            stat_recv.at[panel, head], stat_recv.at[panel, head],
            stat_send_sem.at[head, s], stat_recv_sem.at[panel, head],
            {"ka": ring(panel, s, n_ka)},
        )

    def stat_arrived(head, source):
        remote(
            stat_recv.at[source, head], stat_recv.at[source, head],
            stat_send_sem.at[head, 0], stat_recv_sem.at[source, head],
            {"ka": ring(panel, 1, n_ka)},
        ).wait_recv()

    def part_copy(send, recv, send_sem, recv_sem, head):
        local = lax.rem(head, own_heads)
        return remote(
            send.at[head], recv.at[panel, local], send_sem.at[head], recv_sem.at[panel, local],
            {"ka": head // own_heads},
        )

    def part_arrived(recv, send_sem, recv_sem, source, local):
        remote(
            recv.at[source, local], recv.at[source, local],
            send_sem.at[0], recv_sem.at[source, local], {"ka": ring(panel, 1, n_ka)},
        ).wait_recv()

    def finish_head(i, _):
        head = head_at(i)
        cols = head_columns(head)
        total = run_total[:, cols]
        out = out_acc[:, cols] * (1.0 / total)
        delta = jnp.sum(out * do_turned[:, cols].astype(F32), axis=0, keepdims=True)
        stat_recv[panel, head, 0:1, :] = run_max[:, cols] + jnp.log2(total)
        stat_recv[panel, head, 1:2, :] = delta
        for s in range(1, n_ka):
            stat_copy(head, s).start()

        @pl.when(i < heads - own_heads)
        def _():
            out_send[head] = out.astype(BF16)
            part_copy(out_send, out_recv, out_send_sem, out_recv_sem, head).start()

        @pl.when(i >= heads - own_heads)
        def _():
            out_recv[panel, lax.rem(head, own_heads)] = out.astype(BF16)

        return 0

    lax.fori_loop(0, heads, finish_head, 0)

    def merge_head(i, _):
        head = head_at(i)
        cols = head_columns(head)
        for s in range(1, n_ka):
            stat_arrived(head, ring(panel, s, n_ka))
        lses = [stat_recv[n, head, 0:1, :] for n in range(n_ka)]
        peak = functools.reduce(jnp.maximum, lses)
        lse = peak + jnp.log2(sum(jnp.exp2(one - peak) for one in lses))
        row_lse[:, cols] = lse
        row_delta[:, cols] = sum(
            jnp.exp2(lses[n] - lse) * stat_recv[n, head, 1:2, :] for n in range(n_ka)
        )
        return 0

    lax.fori_loop(0, heads, merge_head, 0)

    def back_group_of(k):
        return ring(z, k + 1, groups)

    def core_sum_copy(k):
        return remote(
            core_send.at[k], core_recv.at[k], core_send_sem.at[k], core_recv_sem.at[k],
            {"pb": core_peer},
        )

    def x_sum_copy(k):
        return remote(
            x_send.at[k], x_recv.at[k], x_send_sem.at[k], x_recv_sem.at[k], {"pb": x_peer}
        )

    def z_sum_copy(k):
        return remote(
            z_send.at[k], z_recv.at[k], z_send_sem.at[k], z_recv_sem.at[k],
            {"pb": at(back_group_of(k), x, core)},
        )

    def send_core(k):
        slot = lax.rem(k, 2)
        for part in range(2):
            core_send[k, part] = acc[slot, 2 * part + other_core].astype(BF16)
        core_sum_copy(k).start()

    def send_x(k):
        slot = lax.rem(k, 2)
        core_sum_copy(k).wait_recv()
        passed = acc[slot, 2 * other_x + core] + core_recv[k, other_x].astype(F32)
        x_send[k] = passed.astype(BF16)
        x_sum_copy(k).start()
        mine = 2 * x + core
        acc[slot, mine] = acc[slot, mine] + core_recv[k, x].astype(F32)

    def x_total(k):
        x_sum_copy(k).wait_recv()
        return acc[lax.rem(k, 2), 2 * x + core] + x_recv[k].astype(F32)

    def send_z(k):
        z_send[k] = x_total(k).astype(BF16)
        z_sum_copy(k).start()

    def backward_group(k, _):
        group = back_group_of(k)
        slot = lax.rem(k, 2)

        def backward_head(i, _):
            head = head_at(i)
            cols = head_columns(head)
            mix = jnp.exp2(group_max[group, :, cols] - row_lse[:, cols])
            dprobs = dot_nn(group_rows(group, chunk), do_turned[:, cols])
            ds = weights[group, :, cols] * (dprobs - row_delta[:, cols]).astype(BF16)
            dscores[:, cols] = ds
            q_scaled[:, cols] = (q_turned[:, cols].astype(F32) * (mix * scale)).astype(BF16)
            do_scaled[:, cols] = (do_turned[:, cols].astype(F32) * mix).astype(BF16)
            dq_acc[:, cols] = dq_acc[:, cols] + dot_nn(k_turned[group], ds) * (mix * scale)

            @pl.when((k == groups - 1) & (i < heads - own_heads))
            def _():
                dq_send[head] = dq_acc[:, cols].astype(BF16)
                part_copy(dq_send, dq_recv, dq_send_sem, dq_recv_sem, head).start()

            return 0

        lax.fori_loop(0, heads // 2, backward_head, 0, unroll=2)

        @pl.when(k > 0)
        def _():
            send_x(k - 1)

        lax.fori_loop(heads // 2, heads, backward_head, 0, unroll=2)

        @pl.when(k > 0)
        def _():
            send_z(k - 1)

        key_part = dot_nt(dscores[...], q_scaled[...])
        value_part = dot_nt(weights[group], do_scaled[...])
        acc[slot, :, 0:chunk, :] = key_part.reshape(4, chunk, dim)
        acc[slot, :, chunk : 2 * chunk, :] = value_part.reshape(4, chunk, dim)
        send_core(k)
        return 0

    lax.fori_loop(0, groups, backward_group, 0)

    for local in range(own_heads):
        head = panel * own_heads + local
        cols = head_columns(head)
        for s in range(1, n_ka):
            part_arrived(out_recv, out_send_sem, out_recv_sem, ring(panel, s, n_ka), local)
        lse = row_lse[:, cols]
        mixed = sum(
            jnp.exp2(stat_recv[n, head, 0:1, :] - lse) * out_recv[n, local].astype(F32)
            for n in range(n_ka)
        )
        att_ref[:, local * dim : (local + 1) * dim] = mixed.T.astype(BF16)
        dq_recv[panel, local] = dq_acc[:, cols].astype(BF16)

    last = groups - 1
    send_x(last)
    total = x_total(last)
    for k in range(last):
        z_sum_copy(k).wait_recv()
        total = total + z_recv[k].astype(F32)
    kg_ref[...] = total[0:chunk]
    vg_ref[...] = total[chunk : 2 * chunk]

    for local in range(own_heads):
        for s in range(1, n_ka):
            part_arrived(dq_recv, dq_send_sem, dq_recv_sem, ring(panel, s, n_ka), local)
        summed = sum(dq_recv[n, local].astype(F32) for n in range(n_ka))
        qg_ref[:, local * dim : (local + 1) * dim] = summed.T

    def drain_group(k, _):
        x_copy(k).wait_send()
        core_copy(k, 0).wait_send()
        core_copy(k, 1).wait_send()
        core_sum_copy(k).wait_send()
        x_sum_copy(k).wait_send()

        @pl.when(k < last)
        def _():
            z_copy(k + 1).wait_send()
            z_sum_copy(k).wait_send()

        return 0

    lax.fori_loop(0, groups, drain_group, 0)

    def drain_head(i, _):
        head = head_at(i)
        for s in range(1, n_ka):
            stat_copy(head, s).wait_send()

        @pl.when(i < heads - own_heads)
        def _():
            part_copy(out_send, out_recv, out_send_sem, out_recv_sem, head).wait_send()
            part_copy(dq_send, dq_recv, dq_send_sem, dq_recv_sem, head).wait_send()

        return 0

    lax.fori_loop(0, heads, drain_head, 0)


def per_device(n_pb, n_ka, queries, keys, values, dout, block_mask):
    rows, width = queries.shape
    chunk, dim = keys.shape
    heads = width // dim
    own_heads = heads // n_ka
    groups = n_pb // 4
    group_keys = 4 * chunk
    wide = heads * rows
    assert rows == 2 * BLOCK and group_keys % BLOCK == 0
    vmem, dma = pltpu.VMEM, pltpu.SemaphoreType.DMA
    pair = (2 * chunk, dim)
    return pl.pallas_call(
        functools.partial(kernel, n_pb, n_ka),
        out_shape=(
            jax.ShapeDtypeStruct((rows, own_heads * dim), BF16),
            jax.ShapeDtypeStruct((rows, own_heads * dim), F32),
            jax.ShapeDtypeStruct((chunk, dim), F32),
            jax.ShapeDtypeStruct((chunk, dim), F32),
        ),
        in_specs=[pl.BlockSpec(memory_space=pltpu.SMEM)]
        + [pl.BlockSpec(memory_space=pltpu.VMEM)] * 4,
        out_specs=[pl.BlockSpec(memory_space=pltpu.VMEM)] * 4,
        scratch_shapes=[
            vmem((n_pb,) + pair, BF16),
            vmem((groups, dim, group_keys), BF16),
            vmem((dim, wide), BF16),
            vmem((dim, wide), BF16),
            vmem((dim, wide), BF16),
            vmem((dim, wide), BF16),
            vmem((groups, group_keys, wide), BF16),
            vmem((group_keys, wide), BF16),
            vmem((dim, wide), F32),
            vmem((dim, wide), F32),
            vmem((1, wide), F32),
            vmem((1, wide), F32),
            vmem((groups, 1, wide), F32),
            vmem((1, wide), F32),
            vmem((1, wide), F32),
            vmem((n_ka, heads, 8, rows), F32),
            vmem((heads, dim, rows), BF16),
            vmem((n_ka, own_heads, dim, rows), BF16),
            vmem((heads, dim, rows), BF16),
            vmem((n_ka, own_heads, dim, rows), BF16),
            vmem((2, 4) + pair, F32),
            vmem((groups, 2) + pair, BF16),
            vmem((groups, 2) + pair, BF16),
            vmem((groups,) + pair, BF16),
            vmem((groups,) + pair, BF16),
            vmem((groups,) + pair, BF16),
            vmem((groups,) + pair, BF16),
            dma((n_pb,)),
            dma((groups,)),
            dma((groups,)),
            dma((2 * groups,)),
            dma((heads, n_ka)),
            dma((n_ka, heads)),
            dma((heads,)),
            dma((n_ka, own_heads)),
            dma((heads,)),
            dma((n_ka, own_heads)),
            dma((groups,)),
            dma((groups,)),
            dma((groups,)),
            dma((groups,)),
            dma((groups,)),
            dma((groups,)),
        ],
        compiler_params=pltpu.CompilerParams(
            collective_id=0, has_side_effects=True, vmem_limit_bytes=52 * 2**20
        ),
        cost_estimate=pl.CostEstimate(
            flops=12 * wide * n_pb * chunk * dim,
            bytes_accessed=4 * rows * width * 2,
            transcendentals=wide * n_pb * chunk,
        ),
    )(block_mask, queries, keys, values, dout)


def solution(mesh):
    in_specs = (
        P("pb", None),
        P(("ka", "pb"), None),
        P(("ka", "pb"), None),
        P("pb", None),
        P("pb", "ka"),
    )
    out_specs = (P("pb", "ka"), P("pb", "ka"), P(("ka", "pb"), None), P(("ka", "pb"), None))
    return jax.shard_map(
        functools.partial(per_device, mesh.shape["pb"], mesh.shape["ka"]),
        mesh=mesh, in_specs=in_specs, out_specs=out_specs, check_vma=False,
    )
```

time: 361 us -> 76.7 us (0.21)
  waiting for transfers between devices: 161 us -> 0 us
  matrix products: 111 us -> 0 us
  Pallas kernels: 0 us -> 69.7 us
  blocking collectives: 48.1 us -> 0 us
  between operations: 14 us -> 0.65 us
  local copies, waits for them, and re-layouts: 15.4 us -> 5.98 us
  other arithmetic: 7.47 us -> 0 us
    reduce_scatter x3 -> x0, waiting for transfers between devices: 133 us -> none  [the longest x1 60.4 us: per_device(): lax.psum_scatter(value_parts.reshape(-1, head_width), 'pb', scatter_dimen...]
    dot_general x128 -> x0, matrix products: 111 us -> none  [the longest x16 40.5 us: compute(): jnp.einsum('hqk,kd->qhd', dscores, key_tile, preferred_element_type=jnp.f...]
    pallas_call x0 -> x1, Pallas kernels: none -> 69.7 us  [per_device(): pl.pallas_call(functools.partial(kernel, n_pb, n_ka), out_shape=(jax.Shap...]
    all_gather x3 -> x0, blocking collectives: 48.1 us -> none  [the longest x1 24.8 us: per_device(): lax.all_gather(keys, 'pb', axis=0, tiled=True)]
    all_gather x1 -> x0, waiting for transfers between devices: 26.7 us -> none  [merged_2(): gathered = jax.tree.map(lambda a: lax.all_gather(a, axis), part)]
    unnamed x16 -> x12, local copies, waits for them, and re-layouts: 7.71 us -> 5.98 us
  transfers between devices with their start and end apart: 4 -> 0, of which waited for: 4 -> 0; matrix products, arithmetic and copies ran while one was open for 1% -> 0% of each run, Pallas kernels for 0% -> 0%
where the time goes in v1:
time: 76.7 us; the launch traced here: 76.4 us
  Pallas kernels  69.7 us (91%)
  local copies, waits for them, and re-layouts  5.98 us (8%)
    pallas_call x1, Pallas kernels, per_device(): pl.pallas_call(functools.partial(kernel, n_pb, n_ka), out_shape=(jax.Shap...  69.7 us
    unnamed x12, local copies, waits for them, and re-layouts  5.98 us

profile of v1, /device:TPU:0, one launch (start us, length us, event | category | flops | bytes accessed | tf_op | source)
XLA Modules:
  0.0 76.4 jit_solution(7812847047046288662)
XLA Ops:
  0.6 0.0 copy-start
  0.6 1.0 %copy-done = bf16[256,1024]{1,0:T(8,128)(2,1)S(1)} copy-done((bf16[256,1024]{1,0:T(8,128)(2,1)S(1)}, bf16[256,1024]{1,0:T(8,128)(2,1)}, u32[]{:S(2)}) %copy-start) | copy-done | bytes 524312
  1.7 0.0 copy-start.1
  1.7 0.8 copy-done.1
  2.4 0.0 copy-start.2
  2.4 0.8 copy-done.2
  3.2 0.0 copy-start.3
  3.2 0.7 copy-done.3
  3.9 69.7 %shard_map.84 = (bf16[256,512]{1,0:T(8,128)(2,1)S(1)}, f32[256,512]{1,0:T(8,128)S(1)}, f32[128,128]{1,0:T(8,128)S(1)}, f32[128,128]{1,0:T(8,128)S(1)}) custom-call(s32[2,16]{1,0:T(2,128)S(1)} %copy-done.3, bf16[256,1024]{1,0:T(8,128)(2,1)S(1)} %copy-done, bf16[128,128]{1,0:T(8,128)(2,1)S(1)} %copy-done.1, bf16[128,128]{1,0:T(8,128)(2,1)S(1)} %copy-done.2, ...), custom_call_target="tpu_custom_call" | custom-call | flops 6442450944 | bytes 2097152 | tf_op jit(solution)/shard_map/pallas_call | solution.py:414
  73.6 0.7 copy.13
  74.3 0.8 %copy.14 = f32[256,512]{1,0:T(8,128)} copy(f32[256,512]{1,0:T(8,128)S(1)} %get-tuple-element.9) | data formatting | bytes 1048576
  75.1 0.6 copy.15
  75.7 0.6 copy.16
Async XLA Ops:
  0.6 1.0 %copy-start = (bf16[256,1024]{1,0:T(8,128)(2,1)S(1)}, bf16[256,1024]{1,0:T(8,128)(2,1)}, u32[]{:S(2)}) copy-start(bf16[256,1024]{1,0:T(8,128)(2,1)} %q_ref.1) | copy-start | bytes 1572868
  1.7 0.8 copy-start.1
  2.4 0.8 copy-start.2
  3.2 0.7 copy-start.3

commit v2 on v1

--- a/solution.py
+++ b/solution.py
@@ -26,11 +26,11 @@
     n_pb, n_ka,
     mask_ref, q_ref, k_ref, v_ref, do_ref,
     att_ref, qg_ref, kg_ref, vg_ref,
-    kv, k_turned, q_turned, do_turned, q_scaled, do_scaled, weights, dscores,
+    kv, k_turned, q_rows, do_rows, q_turned, do_turned, weights, wide_scores, probs, dscores,
     out_acc, dq_acc, run_max, run_total, group_max, row_lse, row_delta,
     stat_recv, out_send, out_recv, dq_send, dq_recv,
     acc, core_send, core_recv, x_send, x_recv, z_send, z_recv,
-    ag_recv_sem, ag_z_sem, ag_x_sem, ag_core_sem,
+    load_sem, ag_recv_sem, ag_z_sem, ag_x_sem, ag_core_sem,
     stat_send_sem, stat_recv_sem, out_send_sem, out_recv_sem, dq_send_sem, dq_recv_sem,
     core_send_sem, core_recv_sem, x_send_sem, x_recv_sem, z_send_sem, z_recv_sem,
 ):
@@ -65,14 +65,33 @@
     def ring(start, step, size):
         return lax.rem(start + step, size)
 
+    def load(index, src, dst):
+        return pltpu.make_async_copy(src, dst, load_sem.at[index])
+
+    loads = [
+        load(0, k_ref, kv.at[me, pl.ds(0, chunk)]),
+        load(1, v_ref, kv.at[me, pl.ds(chunk, chunk)]),
+    ]
+    for part, (src, dst) in enumerate(((q_ref, q_rows), (do_ref, do_rows))):
+        for head in range(heads):
+            loads.append(
+                load(
+                    2 + part * heads + head,
+                    src.at[:, pl.ds(head * dim, dim)],
+                    dst.at[pl.ds(head * rows, rows), :],
+                )
+            )
+    for one in loads:
+        one.start()
+
     barrier = pltpu.get_barrier_semaphore()
     partners = [{"pb": core_peer}, {"pb": x_peer}]
     partners += [{"pb": at(ring(z, s, groups), x, core)} for s in range(1, groups)]
     partners += [{"ka": ring(panel, s, n_ka)} for s in range(1, n_ka)]
     for partner in partners:
         pl.semaphore_signal(barrier, inc=1, device_id=partner, device_id_type=pl.DeviceIdType.MESH)
-    kv[me, 0:chunk, :] = k_ref[...]
-    kv[me, chunk : 2 * chunk, :] = v_ref[...]
+    loads[0].wait()
+    loads[1].wait()
     pl.semaphore_wait(barrier, len(partners))
 
     def gather_copy(index, send_sem, device):
@@ -103,11 +122,12 @@
     def head_at(i):
         return lax.rem((panel + 1) * own_heads + i, heads)
 
+    for one in loads[2:]:
+        one.wait()
     for head in range(heads):
-        source = pl.ds(head * dim, dim)
-        target = pl.ds(head * rows, rows)
-        q_turned[:, target] = q_ref[:, source].T
-        do_turned[:, target] = do_ref[:, source].T
+        span = pl.ds(head * rows, rows)
+        q_turned[:, span] = q_rows[span, :].T
+        do_turned[:, span] = do_rows[span, :].T
     out_acc[...] = jnp.zeros_like(out_acc)
     dq_acc[...] = jnp.zeros_like(dq_acc)
     run_max[...] = jnp.full_like(run_max, -1e38)
@@ -145,40 +165,46 @@
             for b in range(group_blocks)
         ]
 
-        def forward_head(i, _):
-            cols = head_columns(head_at(i))
-            scores = dot_nn(group_rows(group, 0), q_turned[:, cols])
-            parts = [
-                scores[b * BLOCK : (b + 1) * BLOCK] * log_scale + bias[b]
-                for b in range(group_blocks)
-            ]
-            peak = functools.reduce(
-                jnp.maximum, [jnp.max(part, axis=0, keepdims=True) for part in parts]
-            )
-            low = []
-            total = jnp.zeros_like(peak)
-            for part in parts:
-                weight = jnp.exp2(part - peak)
-                total = total + jnp.sum(weight, axis=0, keepdims=True)
-                low.append(weight.astype(BF16))
-            low = jnp.concatenate(low, axis=0)
-            weights[group, :, cols] = low
-            group_max[group, :, cols] = peak
-            old = run_max[:, cols]
-            new = jnp.maximum(old, peak)
-            keep, add = jnp.exp2(old - new), jnp.exp2(peak - new)
-            run_max[:, cols] = new
-            run_total[:, cols] = run_total[:, cols] * keep + total * add
-            out_acc[:, cols] = out_acc[:, cols] * keep + dot_nn(values_turned, low) * add
-            return 0
-
-        lax.fori_loop(0, heads // 2, forward_head, 0, unroll=2)
+        def forward_heads(first, last):
+            def score(i):
+                scores = dot_nn(group_rows(group, 0), q_turned[:, head_columns(head_at(i))])
+                wide_scores[i - first] = scores
+                return [
+                    jnp.max(scores[b * BLOCK : (b + 1) * BLOCK], axis=0, keepdims=True) * log_scale
+                    for b in range(group_blocks)
+                ]
+
+            peaks = score(first)
+            for i in range(first, last):
+                later = score(i + 1) if i + 1 < last else None
+                cols = head_columns(head_at(i))
+                peak = functools.reduce(jnp.maximum, [p + one for p, one in zip(peaks, bias)])
+                low = []
+                total = jnp.zeros_like(peak)
+                for b in range(group_blocks):
+                    shift = jnp.maximum(peak - bias[b], peaks[b])
+                    part = wide_scores[i - first, b * BLOCK : (b + 1) * BLOCK, :]
+                    weight = jnp.exp2(part * log_scale - shift)
+                    total = total + jnp.sum(weight, axis=0, keepdims=True)
+                    low.append(weight.astype(BF16))
+                low = jnp.concatenate(low, axis=0)
+                weights[group, :, cols] = low
+                group_max[group, :, cols] = peak
+                old = run_max[:, cols]
+                new = jnp.maximum(old, peak)
+                keep, add = jnp.exp2(old - new), jnp.exp2(peak - new)
+                run_max[:, cols] = new
+                run_total[:, cols] = run_total[:, cols] * keep + total * add
+                out_acc[:, cols] = out_acc[:, cols] * keep + dot_nn(values_turned, low) * add
+                peaks = later
+
+        forward_heads(0, heads // 2)
 
         @pl.when(more)
         def _():
             stage_x(k + 1)
 
-        lax.fori_loop(heads // 2, heads, forward_head, 0, unroll=2)
+        forward_heads(heads // 2, heads)
 
         @pl.when(more)
         def _():
@@ -302,40 +328,63 @@
         group = back_group_of(k)
         slot = lax.rem(k, 2)
 
-        def backward_head(i, _):
-            head = head_at(i)
-            cols = head_columns(head)
-            mix = jnp.exp2(group_max[group, :, cols] - row_lse[:, cols])
-            dprobs = dot_nn(group_rows(group, chunk), do_turned[:, cols])
-            ds = weights[group, :, cols] * (dprobs - row_delta[:, cols]).astype(BF16)
-            dscores[:, cols] = ds
-            q_scaled[:, cols] = (q_turned[:, cols].astype(F32) * (mix * scale)).astype(BF16)
-            do_scaled[:, cols] = (do_turned[:, cols].astype(F32) * mix).astype(BF16)
-            dq_acc[:, cols] = dq_acc[:, cols] + dot_nn(k_turned[group], ds) * (mix * scale)
-
-            @pl.when((k == groups - 1) & (i < heads - own_heads))
-            def _():
-                dq_send[head] = dq_acc[:, cols].astype(BF16)
+        def rows_of(i):
+            return pl.ds(pl.multiple_of(head_at(i) * rows, rows), rows)
+
+        def backward_heads(first, last):
+            def dprob(i):
+                return dot_nn(group_rows(group, chunk), do_turned[:, head_columns(head_at(i))])
+
+            dprobs = dprob(first)
+            for i in range(first, last):
+                later = dprob(i + 1) if i + 1 < last else None
+                cols = head_columns(head_at(i))
+                mix = jnp.exp2(group_max[group, :, cols] - row_lse[:, cols])
+                low = weights[group, :, cols] * mix.astype(BF16)
+                place = pl.ds(i * rows, rows)
+                probs[:, place] = low
+                ds = low * (dprobs - row_delta[:, cols]).astype(BF16)
+                dscores[:, place] = ds
+                dq_acc[:, cols] = dq_acc[:, cols] + dot_nn(k_turned[group], ds)
+                dprobs = later
+
+        def send_dq(first, last):
+            for i in range(first, min(last, heads - own_heads)):
+                head = head_at(i)
+                dq_send[head] = (dq_acc[:, head_columns(head)] * scale).astype(BF16)
                 part_copy(dq_send, dq_recv, dq_send_sem, dq_recv_sem, head).start()
 
-            return 0
-
-        lax.fori_loop(0, heads // 2, backward_head, 0, unroll=2)
+        def grads(first, last):
+            span = slice(first * rows, last * rows)
+            q_part = jnp.concatenate([q_rows[rows_of(i), :] for i in range(first, last)], axis=0)
+            do_part = jnp.concatenate([do_rows[rows_of(i), :] for i in range(first, last)], axis=0)
+            return dot_nn(dscores[:, span], q_part), dot_nn(probs[:, span], do_part)
+
+        half = heads // 2
+        backward_heads(0, half)
+
+        @pl.when(k == groups - 1)
+        def _():
+            send_dq(0, half)
 
         @pl.when(k > 0)
         def _():
             send_x(k - 1)
 
-        lax.fori_loop(heads // 2, heads, backward_head, 0, unroll=2)
+        key_part, value_part = grads(0, half)
+        backward_heads(half, heads)
+        key_more, value_more = grads(half, heads)
+
+        @pl.when(k == groups - 1)
+        def _():
+            send_dq(half, heads)
 
         @pl.when(k > 0)
         def _():
             send_z(k - 1)
 
-        key_part = dot_nt(dscores[...], q_scaled[...])
-        value_part = dot_nt(weights[group], do_scaled[...])
-        acc[slot, :, 0:chunk, :] = key_part.reshape(4, chunk, dim)
-        acc[slot, :, chunk : 2 * chunk, :] = value_part.reshape(4, chunk, dim)
+        acc[slot, :, 0:chunk, :] = ((key_part + key_more) * scale).reshape(4, chunk, dim)
+        acc[slot, :, chunk : 2 * chunk, :] = (value_part + value_more).reshape(4, chunk, dim)
         send_core(k)
         return 0
 
@@ -352,7 +401,7 @@
             for n in range(n_ka)
         )
         att_ref[:, local * dim : (local + 1) * dim] = mixed.T.astype(BF16)
-        dq_recv[panel, local] = dq_acc[:, cols].astype(BF16)
+        dq_recv[panel, local] = (dq_acc[:, cols] * scale).astype(BF16)
 
     last = groups - 1
     send_x(last)
@@ -398,6 +447,15 @@
         return 0
 
     lax.fori_loop(0, heads, drain_head, 0)
+
+
+def hand_over(a, b, c, d, a_out, b_out, c_out, d_out, sem):
+    pairs = ((a, a_out), (b, b_out), (c, c_out), (d, d_out))
+    copies = [pltpu.make_async_copy(src, dst, sem.at[i]) for i, (src, dst) in enumerate(pairs)]
+    for copy in copies:
+        copy.start()
+    for copy in copies:
+        copy.wait()
 
 
 def per_device(n_pb, n_ka, queries, keys, values, dout, block_mask):
@@ -411,7 +469,7 @@
     assert rows == 2 * BLOCK and group_keys % BLOCK == 0
     vmem, dma = pltpu.VMEM, pltpu.SemaphoreType.DMA
     pair = (2 * chunk, dim)
-    return pl.pallas_call(
+    results = pl.pallas_call(
         functools.partial(kernel, n_pb, n_ka),
         out_shape=(
             jax.ShapeDtypeStruct((rows, own_heads * dim), BF16),
@@ -420,16 +478,18 @@
             jax.ShapeDtypeStruct((chunk, dim), F32),
         ),
         in_specs=[pl.BlockSpec(memory_space=pltpu.SMEM)]
-        + [pl.BlockSpec(memory_space=pltpu.VMEM)] * 4,
+        + [pl.BlockSpec(memory_space=pl.ANY)] * 4,
         out_specs=[pl.BlockSpec(memory_space=pltpu.VMEM)] * 4,
         scratch_shapes=[
             vmem((n_pb,) + pair, BF16),
             vmem((groups, dim, group_keys), BF16),
-            vmem((dim, wide), BF16),
-            vmem((dim, wide), BF16),
+            vmem((wide, dim), BF16),
+            vmem((wide, dim), BF16),
             vmem((dim, wide), BF16),
             vmem((dim, wide), BF16),
             vmem((groups, group_keys, wide), BF16),
+            vmem((heads // 2, group_keys, rows), F32),
+            vmem((group_keys, wide), BF16),
             vmem((group_keys, wide), BF16),
             vmem((dim, wide), F32),
             vmem((dim, wide), F32),
@@ -450,6 +510,7 @@
             vmem((groups,) + pair, BF16),
             vmem((groups,) + pair, BF16),
             vmem((groups,) + pair, BF16),
+            dma((2 + 2 * heads,)),
             dma((n_pb,)),
             dma((groups,)),
             dma((groups,)),
@@ -468,7 +529,7 @@
             dma((groups,)),
         ],
         compiler_params=pltpu.CompilerParams(
-            collective_id=0, has_side_effects=True, vmem_limit_bytes=52 * 2**20
+            collective_id=0, has_side_effects=True, vmem_limit_bytes=58 * 2**20
         ),
         cost_estimate=pl.CostEstimate(
             flops=12 * wide * n_pb * chunk * dim,
@@ -476,6 +537,14 @@
             transcendentals=wide * n_pb * chunk,
         ),
     )(block_mask, queries, keys, values, dout)
+    return pl.pallas_call(
+        hand_over,
+        out_shape=tuple(jax.ShapeDtypeStruct(one.shape, one.dtype) for one in results),
+        in_specs=[pl.BlockSpec(memory_space=pl.ANY)] * 4,
+        out_specs=[pl.BlockSpec(memory_space=pl.ANY)] * 4,
+        scratch_shapes=[dma((4,))],
+        compiler_params=pltpu.CompilerParams(vmem_limit_bytes=63 * 2**20),
+    )(*results)
 
 
 def solution(mesh):

time: 76.7 us -> 92.7 us (1.21)
  Pallas kernels: 69.7 us -> 91.9 us
  local copies, waits for them, and re-layouts: 5.98 us -> 0 us
    pallas_call x0 -> x1, Pallas kernels: none -> 28.9 us  [per_device(): pl.pallas_call(hand_over, out_shape=tuple((jax.ShapeDtypeStruct(one.shape...]
    pallas_call x1, Pallas kernels: 69.7 us -> 63 us  [per_device(): pl.pallas_call(functools.partial(kernel, n_pb, n_ka), out_shape=(jax.Shap...]
    unnamed x12 -> x0, local copies, waits for them, and re-layouts: 5.98 us -> none
where the time goes in v2:
time: 92.7 us; the launch traced here: 92.5 us
  Pallas kernels  91.9 us (99%)
    pallas_call x1, Pallas kernels, per_device(): pl.pallas_call(functools.partial(kernel, n_pb, n_ka), out_shape=(jax.Shap...  63 us
    pallas_call x1, Pallas kernels, per_device(): pl.pallas_call(hand_over, out_shape=tuple((jax.ShapeDtypeStruct(one.shape...  28.9 us

profile of v2, /device:TPU:0, one launch (start us, length us, event | category | flops | bytes accessed | tf_op | source)
XLA Modules:
  0.0 92.5 jit_solution(5036272381076919425)
XLA Ops:
  0.6 63.0 %shard_map.84 = (bf16[256,512]{1,0:T(8,128)(2,1)}, f32[256,512]{1,0:T(8,128)}, f32[128,128]{1,0:T(8,128)}, f32[128,128]{1,0:T(8,128)}) custom-call(s32[2,16]{1,0:T(2,128)} %mask_ref.1, bf16[256,1024]{1,0:T(8,128)(2,1)} %q_ref.1, bf16[128,128]{1,0:T(8,128)(2,1)} %k_ref.1, bf16[128,128]{1,0:T(8,128)(2,1)} %v_ref.1, bf16[256,1024]{1,0:T(8,128)(2,1)} %do_ref.1), custom_call_target="tpu_custom_call" | custom-call | flops 6442450944 | bytes 2097152 | tf_op jit(solution)/shard_map/pallas_call | solution.py:472
  63.6 28.9 %shard_map.85 = (bf16[256,512]{1,0:T(8,128)(2,1)}, f32[256,512]{1,0:T(8,128)}, f32[128,128]{1,0:T(8,128)}, f32[128,128]{1,0:T(8,128)}) custom-call(bf16[256,512]{1,0:T(8,128)(2,1)} %get-tuple-element.8.a, f32[256,512]{1,0:T(8,128)} %get-tuple-element.9.b, f32[128,128]{1,0:T(8,128)} %get-tuple-element.10.c, f32[128,128]{1,0:T(8,128)} %get-tuple-element.11.d), custom_call_target="tpu_custom_call" | custom-call | tf_op jit(solution)/shard_map/pallas_call | solution.py:540

commit v3 on v2

--- a/solution.py
+++ b/solution.py
@@ -116,11 +116,14 @@
     for s in range(1, groups):
         z_copy(s).start()
 
-    def head_columns(head):
-        return pl.ds(pl.multiple_of(head * rows, rows), rows)
+    def head_columns(head, count=1):
+        return pl.ds(pl.multiple_of(head * rows, rows), count * rows)
 
     def head_at(i):
-        return lax.rem((panel + 1) * own_heads + i, heads)
+        return lax.rem((panel + 1) * own_heads + i, heads) if own_heads % 2 == 0 else i
+
+    def foreign(head):
+        return head // own_heads != panel
 
     for one in loads[2:]:
         one.wait()
@@ -167,23 +170,23 @@
 
         def forward_heads(first, last):
             def score(i):
-                scores = dot_nn(group_rows(group, 0), q_turned[:, head_columns(head_at(i))])
-                wide_scores[i - first] = scores
+                scores = dot_nn(group_rows(group, 0), q_turned[:, head_columns(head_at(i), 2)])
+                wide_scores[(i - first) // 2] = scores
                 return [
                     jnp.max(scores[b * BLOCK : (b + 1) * BLOCK], axis=0, keepdims=True) * log_scale
                     for b in range(group_blocks)
                 ]
 
             peaks = score(first)
-            for i in range(first, last):
-                later = score(i + 1) if i + 1 < last else None
-                cols = head_columns(head_at(i))
+            for i in range(first, last, 2):
+                later = score(i + 2) if i + 2 < last else None
+                cols = head_columns(head_at(i), 2)
                 peak = functools.reduce(jnp.maximum, [p + one for p, one in zip(peaks, bias)])
                 low = []
                 total = jnp.zeros_like(peak)
                 for b in range(group_blocks):
                     shift = jnp.maximum(peak - bias[b], peaks[b])
-                    part = wide_scores[i - first, b * BLOCK : (b + 1) * BLOCK, :]
+                    part = wide_scores[(i - first) // 2, b * BLOCK : (b + 1) * BLOCK, :]
                     weight = jnp.exp2(part * log_scale - shift)
                     total = total + jnp.sum(weight, axis=0, keepdims=True)
                     low.append(weight.astype(BF16))
@@ -252,12 +255,12 @@
         for s in range(1, n_ka):
             stat_copy(head, s).start()
 
-        @pl.when(i < heads - own_heads)
+        @pl.when(foreign(head))
         def _():
             out_send[head] = out.astype(BF16)
             part_copy(out_send, out_recv, out_send_sem, out_recv_sem, head).start()
 
-        @pl.when(i >= heads - own_heads)
+        @pl.when(jnp.logical_not(foreign(head)))
         def _():
             out_recv[panel, lax.rem(head, own_heads)] = out.astype(BF16)
 
@@ -332,27 +335,35 @@
             return pl.ds(pl.multiple_of(head_at(i) * rows, rows), rows)
 
         def backward_heads(first, last):
-            def dprob(i):
-                return dot_nn(group_rows(group, chunk), do_turned[:, head_columns(head_at(i))])
-
-            dprobs = dprob(first)
-            for i in range(first, last):
-                later = dprob(i + 1) if i + 1 < last else None
-                cols = head_columns(head_at(i))
+            def add_dq(i):
+                cols = head_columns(head_at(i), 2)
+                ds = dscores[:, i * rows : (i + 2) * rows]
+                dq_acc[:, cols] = dq_acc[:, cols] + dot_nn(k_turned[group], ds)
+
+            for i in range(first, last, 2):
+                cols = head_columns(head_at(i), 2)
+                place = slice(i * rows, (i + 2) * rows)
                 mix = jnp.exp2(group_max[group, :, cols] - row_lse[:, cols])
+                dprobs = dot_nn(group_rows(group, chunk), do_turned[:, cols])
                 low = weights[group, :, cols] * mix.astype(BF16)
-                place = pl.ds(i * rows, rows)
                 probs[:, place] = low
-                ds = low * (dprobs - row_delta[:, cols]).astype(BF16)
-                dscores[:, place] = ds
-                dq_acc[:, cols] = dq_acc[:, cols] + dot_nn(k_turned[group], ds)
-                dprobs = later
+                dscores[:, place] = low * (dprobs - row_delta[:, cols]).astype(BF16)
+                if i > first:
+                    add_dq(i - 2)
+            add_dq(last - 2)
 
         def send_dq(first, last):
-            for i in range(first, min(last, heads - own_heads)):
+            def send(i, _):
                 head = head_at(i)
-                dq_send[head] = (dq_acc[:, head_columns(head)] * scale).astype(BF16)
-                part_copy(dq_send, dq_recv, dq_send_sem, dq_recv_sem, head).start()
+
+                @pl.when(foreign(head))
+                def _():
+                    dq_send[head] = (dq_acc[:, head_columns(head)] * scale).astype(BF16)
+                    part_copy(dq_send, dq_recv, dq_send_sem, dq_recv_sem, head).start()
+
+                return 0
+
+            lax.fori_loop(first, last, send, 0)
 
         def grads(first, last):
             span = slice(first * rows, last * rows)
@@ -439,7 +450,7 @@
         for s in range(1, n_ka):
             stat_copy(head, s).wait_send()
 
-        @pl.when(i < heads - own_heads)
+        @pl.when(foreign(head))
         def _():
             part_copy(out_send, out_recv, out_send_sem, out_recv_sem, head).wait_send()
             part_copy(dq_send, dq_recv, dq_send_sem, dq_recv_sem, head).wait_send()
@@ -466,7 +477,7 @@
     groups = n_pb // 4
     group_keys = 4 * chunk
     wide = heads * rows
-    assert rows == 2 * BLOCK and group_keys % BLOCK == 0
+    assert rows == 2 * BLOCK and heads % 4 == 0 and group_keys % BLOCK == 0
     vmem, dma = pltpu.VMEM, pltpu.SemaphoreType.DMA
     pair = (2 * chunk, dim)
     results = pl.pallas_call(
@@ -488,7 +499,7 @@
             vmem((dim, wide), BF16),
             vmem((dim, wide), BF16),
             vmem((groups, group_keys, wide), BF16),
-            vmem((heads // 2, group_keys, rows), F32),
+            vmem((heads // 4, group_keys, 2 * rows), F32),
             vmem((group_keys, wide), BF16),
             vmem((group_keys, wide), BF16),
             vmem((dim, wide), F32),
@@ -541,7 +552,7 @@
         hand_over,
         out_shape=tuple(jax.ShapeDtypeStruct(one.shape, one.dtype) for one in results),
         in_specs=[pl.BlockSpec(memory_space=pl.ANY)] * 4,
-        out_specs=[pl.BlockSpec(memory_space=pl.ANY)] * 4,
+        out_specs=[pl.BlockSpec(memory_space=pltpu.VMEM)] * 4,
         scratch_shapes=[dma((4,))],
         compiler_params=pltpu.CompilerParams(vmem_limit_bytes=63 * 2**20),
     )(*results)

time: 92.7 us -> 65.1 us (0.70)
  Pallas kernels: 91.9 us -> 64.2 us
    pallas_call x1, Pallas kernels: 28.9 us -> 2.07 us  [per_device(): pl.pallas_call(hand_over, out_shape=tuple((jax.ShapeDtypeStruct(one.shape...]
where the time goes in v3:
time: 65.1 us; the launch traced here: 64.9 us
  Pallas kernels  64.2 us (99%)
    pallas_call x1, Pallas kernels, per_device(): pl.pallas_call(functools.partial(kernel, n_pb, n_ka), out_shape=(jax.Shap...  62.1 us
    pallas_call x1, Pallas kernels, per_device(): pl.pallas_call(hand_over, out_shape=tuple((jax.ShapeDtypeStruct(one.shape...  2.07 us

profile of v3, /device:TPU:0, one launch (start us, length us, event | category | flops | bytes accessed | tf_op | source)
XLA Modules:
  0.0 64.9 jit_solution(15836034514110397788)
XLA Ops:
  0.6 62.1 %shard_map.84 = (bf16[256,512]{1,0:T(8,128)(2,1)}, f32[256,512]{1,0:T(8,128)}, f32[128,128]{1,0:T(8,128)}, f32[128,128]{1,0:T(8,128)}) custom-call(s32[2,16]{1,0:T(2,128)} %mask_ref.1, bf16[256,1024]{1,0:T(8,128)(2,1)} %q_ref.1, bf16[128,128]{1,0:T(8,128)(2,1)} %k_ref.1, bf16[128,128]{1,0:T(8,128)(2,1)} %v_ref.1, bf16[256,1024]{1,0:T(8,128)(2,1)} %do_ref.1), custom_call_target="tpu_custom_call" | custom-call | flops 6442450944 | bytes 2097152 | tf_op jit(solution)/shard_map/pallas_call | solution.py:483
  62.8 2.1 %shard_map.85 = (bf16[256,512]{1,0:T(8,128)(2,1)}, f32[256,512]{1,0:T(8,128)}, f32[128,128]{1,0:T(8,128)}, f32[128,128]{1,0:T(8,128)}) custom-call(bf16[256,512]{1,0:T(8,128)(2,1)} %get-tuple-element.8.a, f32[256,512]{1,0:T(8,128)} %get-tuple-element.9.b, f32[128,128]{1,0:T(8,128)} %get-tuple-element.10.c, f32[128,128]{1,0:T(8,128)} %get-tuple-element.11.d), custom_call_target="tpu_custom_call" | custom-call | tf_op jit(solution)/shard_map/pallas_call | solution.py:551

commit v4 on v3

--- a/solution.py
+++ b/solution.py
@@ -125,12 +125,6 @@
     def foreign(head):
         return head // own_heads != panel
 
-    for one in loads[2:]:
-        one.wait()
-    for head in range(heads):
-        span = pl.ds(head * rows, rows)
-        q_turned[:, span] = q_rows[span, :].T
-        do_turned[:, span] = do_rows[span, :].T
     out_acc[...] = jnp.zeros_like(out_acc)
     dq_acc[...] = jnp.zeros_like(dq_acc)
     run_max[...] = jnp.full_like(run_max, -1e38)
@@ -144,7 +138,15 @@
         arrived(at(ring(z, k, groups), x, other_core))
         arrived(at(ring(z, k, groups), other_x, other_core))
 
+    def turn(src, dst, first):
+        for head in range(heads):
+            loads[first + head].wait()
+            span = pl.ds(head * rows, rows)
+            dst[:, span] = src[span, :].T
+
+    turn(q_rows, q_turned, 2)
     stage_x(0)
+    turn(do_rows, do_turned, 2 + heads)
     stage_core(0)
 
     def group_rows(group, first):
@@ -244,29 +246,35 @@
             send_sem.at[0], recv_sem.at[source, local], {"ka": ring(panel, 1, n_ka)},
         ).wait_recv()
 
-    def finish_head(i, _):
+    def finish_stats(i, _):
         head = head_at(i)
         cols = head_columns(head)
         total = run_total[:, cols]
-        out = out_acc[:, cols] * (1.0 / total)
-        delta = jnp.sum(out * do_turned[:, cols].astype(F32), axis=0, keepdims=True)
+        delta = jnp.sum(out_acc[:, cols] * do_turned[:, cols].astype(F32), axis=0, keepdims=True)
         stat_recv[panel, head, 0:1, :] = run_max[:, cols] + jnp.log2(total)
-        stat_recv[panel, head, 1:2, :] = delta
+        stat_recv[panel, head, 1:2, :] = delta / total
         for s in range(1, n_ka):
             stat_copy(head, s).start()
+        return 0
+
+    def finish_out(i, _):
+        head = head_at(i)
+        cols = head_columns(head)
+        out = (out_acc[:, cols] * (1.0 / run_total[:, cols])).astype(BF16)
 
         @pl.when(foreign(head))
         def _():
-            out_send[head] = out.astype(BF16)
+            out_send[head] = out
             part_copy(out_send, out_recv, out_send_sem, out_recv_sem, head).start()
 
         @pl.when(jnp.logical_not(foreign(head)))
         def _():
-            out_recv[panel, lax.rem(head, own_heads)] = out.astype(BF16)
-
-        return 0
-
-    lax.fori_loop(0, heads, finish_head, 0)
+            out_recv[panel, lax.rem(head, own_heads)] = out
+
+        return 0
+
+    lax.fori_loop(0, heads, finish_stats, 0)
+    lax.fori_loop(0, heads, finish_out, 0)
 
     def merge_head(i, _):
         head = head_at(i)
@@ -282,7 +290,8 @@
         )
         return 0
 
-    lax.fori_loop(0, heads, merge_head, 0)
+    half = heads // 2
+    lax.fori_loop(0, half, merge_head, 0)
 
     def back_group_of(k):
         return ring(z, k + 1, groups)
@@ -305,31 +314,28 @@
         )
 
     def send_core(k):
-        slot = lax.rem(k, 2)
         for part in range(2):
-            core_send[k, part] = acc[slot, 2 * part + other_core].astype(BF16)
+            core_send[k, part] = acc[k, 2 * part + other_core].astype(BF16)
         core_sum_copy(k).start()
 
     def send_x(k):
-        slot = lax.rem(k, 2)
         core_sum_copy(k).wait_recv()
-        passed = acc[slot, 2 * other_x + core] + core_recv[k, other_x].astype(F32)
+        passed = acc[k, 2 * other_x + core] + core_recv[k, other_x].astype(F32)
         x_send[k] = passed.astype(BF16)
         x_sum_copy(k).start()
         mine = 2 * x + core
-        acc[slot, mine] = acc[slot, mine] + core_recv[k, x].astype(F32)
+        acc[k, mine] = acc[k, mine] + core_recv[k, x].astype(F32)
 
     def x_total(k):
         x_sum_copy(k).wait_recv()
-        return acc[lax.rem(k, 2), 2 * x + core] + x_recv[k].astype(F32)
+        return acc[k, 2 * x + core] + x_recv[k].astype(F32)
 
     def send_z(k):
         z_send[k] = x_total(k).astype(BF16)
         z_sum_copy(k).start()
 
-    def backward_group(k, _):
+    def backward_block(k, first, last):
         group = back_group_of(k)
-        slot = lax.rem(k, 2)
 
         def rows_of(i):
             return pl.ds(pl.multiple_of(head_at(i) * rows, rows), rows)
@@ -352,54 +358,55 @@
                     add_dq(i - 2)
             add_dq(last - 2)
 
-        def send_dq(first, last):
-            def send(i, _):
-                head = head_at(i)
-
-                @pl.when(foreign(head))
-                def _():
-                    dq_send[head] = (dq_acc[:, head_columns(head)] * scale).astype(BF16)
-                    part_copy(dq_send, dq_recv, dq_send_sem, dq_recv_sem, head).start()
-
-                return 0
-
-            lax.fori_loop(first, last, send, 0)
-
-        def grads(first, last):
-            span = slice(first * rows, last * rows)
-            q_part = jnp.concatenate([q_rows[rows_of(i), :] for i in range(first, last)], axis=0)
-            do_part = jnp.concatenate([do_rows[rows_of(i), :] for i in range(first, last)], axis=0)
-            return dot_nn(dscores[:, span], q_part), dot_nn(probs[:, span], do_part)
-
-        half = heads // 2
-        backward_heads(0, half)
-
-        @pl.when(k == groups - 1)
-        def _():
-            send_dq(0, half)
+        backward_heads(first, last)
+        span = slice(first * rows, last * rows)
+        q_part = jnp.concatenate([q_rows[rows_of(i), :] for i in range(first, last)], axis=0)
+        do_part = jnp.concatenate([do_rows[rows_of(i), :] for i in range(first, last)], axis=0)
+        key_part = dot_nn(dscores[:, span], q_part) * scale
+        value_part = dot_nn(probs[:, span], do_part)
+        return key_part.reshape(4, chunk, dim), value_part.reshape(4, chunk, dim)
+
+    def send_dq(i, _):
+        head = head_at(i)
+
+        @pl.when(foreign(head))
+        def _():
+            dq_send[head] = (dq_acc[:, head_columns(head)] * scale).astype(BF16)
+            part_copy(dq_send, dq_recv, dq_send_sem, dq_recv_sem, head).start()
+
+        return 0
+
+    def sweep_one(k, _):
+        key_part, value_part = backward_block(k, 0, half)
+        acc[k, :, 0:chunk, :] = key_part
+        acc[k, :, chunk : 2 * chunk, :] = value_part
+        return 0
+
+    def sweep_two(k, _):
+        key_part, value_part = backward_block(k, half, heads)
+        acc[k, :, 0:chunk, :] = acc[k, :, 0:chunk, :] + key_part
+        acc[k, :, chunk : 2 * chunk, :] = acc[k, :, chunk : 2 * chunk, :] + value_part
+        send_core(k)
 
         @pl.when(k > 0)
         def _():
             send_x(k - 1)
 
-        key_part, value_part = grads(0, half)
-        backward_heads(half, heads)
-        key_more, value_more = grads(half, heads)
-
-        @pl.when(k == groups - 1)
-        def _():
-            send_dq(half, heads)
-
-        @pl.when(k > 0)
-        def _():
-            send_z(k - 1)
-
-        acc[slot, :, 0:chunk, :] = ((key_part + key_more) * scale).reshape(4, chunk, dim)
-        acc[slot, :, chunk : 2 * chunk, :] = (value_part + value_more).reshape(4, chunk, dim)
-        send_core(k)
-        return 0
-
-    lax.fori_loop(0, groups, backward_group, 0)
+        @pl.when(k > 1)
+        def _():
+            send_z(k - 2)
+
+        return 0
+
+    lax.fori_loop(0, groups, sweep_one, 0)
+    lax.fori_loop(0, half, send_dq, 0)
+    lax.fori_loop(half, heads, merge_head, 0)
+    lax.fori_loop(0, groups, sweep_two, 0)
+    lax.fori_loop(half, heads, send_dq, 0)
+    last = groups - 1
+    if groups > 1:
+        send_z(last - 1)
+    send_x(last)
 
     for local in range(own_heads):
         head = panel * own_heads + local
@@ -414,8 +421,6 @@
         att_ref[:, local * dim : (local + 1) * dim] = mixed.T.astype(BF16)
         dq_recv[panel, local] = (dq_acc[:, cols] * scale).astype(BF16)
 
-    last = groups - 1
-    send_x(last)
     total = x_total(last)
     for k in range(last):
         z_sum_copy(k).wait_recv()
@@ -514,7 +519,7 @@
             vmem((n_ka, own_heads, dim, rows), BF16),
             vmem((heads, dim, rows), BF16),
             vmem((n_ka, own_heads, dim, rows), BF16),
-            vmem((2, 4) + pair, F32),
+            vmem((groups, 4) + pair, F32),
             vmem((groups, 2) + pair, BF16),
             vmem((groups, 2) + pair, BF16),
             vmem((groups,) + pair, BF16),

time: 65.1 us -> 56.6 us (0.87)
  Pallas kernels: 64.2 us -> 55.8 us
    pallas_call x1, Pallas kernels: 62.1 us -> 53.7 us  [per_device(): pl.pallas_call(functools.partial(kernel, n_pb, n_ka), out_shape=(jax.Shap...]
where the time goes in v4:
time: 56.6 us; the launch traced here: 56.4 us
  Pallas kernels  55.8 us (99%)
  between operations  0.64 us (1%)
    pallas_call x1, Pallas kernels, per_device(): pl.pallas_call(functools.partial(kernel, n_pb, n_ka), out_shape=(jax.Shap...  53.7 us
    pallas_call x1, Pallas kernels, per_device(): pl.pallas_call(hand_over, out_shape=tuple((jax.ShapeDtypeStruct(one.shape...  2.07 us

profile of v4, /device:TPU:0, one launch (start us, length us, event | category | flops | bytes accessed | tf_op | source)
XLA Modules:
  0.0 56.4 jit_solution(16333696980584843864)
XLA Ops:
  0.6 53.7 %shard_map.84 = (bf16[256,512]{1,0:T(8,128)(2,1)}, f32[256,512]{1,0:T(8,128)}, f32[128,128]{1,0:T(8,128)}, f32[128,128]{1,0:T(8,128)}) custom-call(s32[2,16]{1,0:T(2,128)} %mask_ref.1, bf16[256,1024]{1,0:T(8,128)(2,1)} %q_ref.1, bf16[128,128]{1,0:T(8,128)(2,1)} %k_ref.1, bf16[128,128]{1,0:T(8,128)(2,1)} %v_ref.1, bf16[256,1024]{1,0:T(8,128)(2,1)} %do_ref.1), custom_call_target="tpu_custom_call" | custom-call | flops 6442450944 | bytes 2097152 | tf_op jit(solution)/shard_map/pallas_call | solution.py:488
  54.3 2.1 %shard_map.85 = (bf16[256,512]{1,0:T(8,128)(2,1)}, f32[256,512]{1,0:T(8,128)}, f32[128,128]{1,0:T(8,128)}, f32[128,128]{1,0:T(8,128)}) custom-call(bf16[256,512]{1,0:T(8,128)(2,1)} %get-tuple-element.8.a, f32[256,512]{1,0:T(8,128)} %get-tuple-element.9.b, f32[128,128]{1,0:T(8,128)} %get-tuple-element.10.c, f32[128,128]{1,0:T(8,128)} %get-tuple-element.11.d), custom_call_target="tpu_custom_call" | custom-call | tf_op jit(solution)/shard_map/pallas_call | solution.py:556

commit v5 on v4

--- a/solution.py
+++ b/solution.py
@@ -152,16 +152,13 @@
     def group_rows(group, first):
         return kv[pl.ds(group * 4, 4), first : first + chunk, :].reshape(group_keys, dim)
 
-    def forward_group(k, _):
+    def stage_z(k):
+        arrived(at(ring(z, k, groups), x, core))
+        x_copy(k).start()
+        core_copy(k, 0).start()
+
+    def forward_group(k, middle=None):
         group = ring(z, k, groups)
-        more = k < groups - 1
-
-        @pl.when(more)
-        def _():
-            arrived(at(ring(z, k + 1, groups), x, core))
-            x_copy(k + 1).start()
-            core_copy(k + 1, 0).start()
-
         keys = group_rows(group, 0)
         k_turned[group] = keys.T
         values_turned = group_rows(group, chunk).T
@@ -203,21 +200,38 @@
                 out_acc[:, cols] = out_acc[:, cols] * keep + dot_nn(values_turned, low) * add
                 peaks = later
 
-        forward_heads(0, heads // 2)
-
-        @pl.when(more)
+        if middle is None:
+            forward_heads(0, heads)
+        else:
+            forward_heads(0, heads // 2)
+            middle()
+            forward_heads(heads // 2, heads)
+
+    def later_group(k, _):
+        @pl.when(k + 2 < groups)
+        def _():
+            stage_z(k + 2)
+
+        @pl.when(k + 1 < groups)
         def _():
             stage_x(k + 1)
 
-        forward_heads(heads // 2, heads)
-
-        @pl.when(more)
+        forward_group(k)
+
+        @pl.when(k + 1 < groups)
         def _():
             stage_core(k + 1)
 
         return 0
 
-    lax.fori_loop(0, groups, forward_group, 0)
+    for k in range(1, min(3, groups)):
+        stage_z(k)
+    if groups > 1:
+        forward_group(0, lambda: stage_x(1))
+        stage_core(1)
+        lax.fori_loop(1, groups, later_group, 0)
+    else:
+        forward_group(0)
 
     def stat_copy(head, s):
         return remote(
@@ -334,36 +348,38 @@
         z_send[k] = x_total(k).astype(BF16)
         z_sum_copy(k).start()
 
-    def backward_block(k, first, last):
+    def backward_block(k, first, last, middle=lambda: None):
         group = back_group_of(k)
+        sums = []
 
         def rows_of(i):
-            return pl.ds(pl.multiple_of(head_at(i) * rows, rows), rows)
-
-        def backward_heads(first, last):
-            def add_dq(i):
-                cols = head_columns(head_at(i), 2)
-                ds = dscores[:, i * rows : (i + 2) * rows]
-                dq_acc[:, cols] = dq_acc[:, cols] + dot_nn(k_turned[group], ds)
-
-            for i in range(first, last, 2):
-                cols = head_columns(head_at(i), 2)
-                place = slice(i * rows, (i + 2) * rows)
-                mix = jnp.exp2(group_max[group, :, cols] - row_lse[:, cols])
-                dprobs = dot_nn(group_rows(group, chunk), do_turned[:, cols])
-                low = weights[group, :, cols] * mix.astype(BF16)
-                probs[:, place] = low
-                dscores[:, place] = low * (dprobs - row_delta[:, cols]).astype(BF16)
-                if i > first:
-                    add_dq(i - 2)
-            add_dq(last - 2)
-
-        backward_heads(first, last)
-        span = slice(first * rows, last * rows)
-        q_part = jnp.concatenate([q_rows[rows_of(i), :] for i in range(first, last)], axis=0)
-        do_part = jnp.concatenate([do_rows[rows_of(i), :] for i in range(first, last)], axis=0)
-        key_part = dot_nn(dscores[:, span], q_part) * scale
-        value_part = dot_nn(probs[:, span], do_part)
+            return pl.ds(pl.multiple_of(head_at(i) * rows, rows), 2 * rows)
+
+        def products(i):
+            cols = head_columns(head_at(i), 2)
+            place = slice(i * rows, (i + 2) * rows)
+            dq_acc[:, cols] = dq_acc[:, cols] + dot_nn(k_turned[group], dscores[:, place])
+            sums.append(
+                (
+                    dot_nn(dscores[:, place], q_rows[rows_of(i), :]),
+                    dot_nn(probs[:, place], do_rows[rows_of(i), :]),
+                )
+            )
+
+        for i in range(first, last, 2):
+            cols = head_columns(head_at(i), 2)
+            place = slice(i * rows, (i + 2) * rows)
+            mix = jnp.exp2(group_max[group, :, cols] - row_lse[:, cols])
+            dprobs = dot_nn(group_rows(group, chunk), do_turned[:, cols])
+            if i > first:
+                products(i - 2)
+            low = weights[group, :, cols] * mix.astype(BF16)
+            probs[:, place] = low
+            dscores[:, place] = low * (dprobs - row_delta[:, cols]).astype(BF16)
+        middle()
+        products(last - 2)
+        key_part = sum(one[0] for one in sums) * scale
+        value_part = sum(one[1] for one in sums)
         return key_part.reshape(4, chunk, dim), value_part.reshape(4, chunk, dim)
 
     def send_dq(i, _):
@@ -383,22 +399,22 @@
         return 0
 
     def sweep_two(k, _):
-        key_part, value_part = backward_block(k, half, heads)
+        def middle():
+            @pl.when(k > 0)
+            def _():
+                send_x(k - 1)
+
+            @pl.when(k > 1)
+            def _():
+                send_z(k - 2)
+
+        key_part, value_part = backward_block(k, half, heads, middle)
         acc[k, :, 0:chunk, :] = acc[k, :, 0:chunk, :] + key_part
         acc[k, :, chunk : 2 * chunk, :] = acc[k, :, chunk : 2 * chunk, :] + value_part
         send_core(k)
-
-        @pl.when(k > 0)
-        def _():
-            send_x(k - 1)
-
-        @pl.when(k > 1)
-        def _():
-            send_z(k - 2)
-
-        return 0
-
-    lax.fori_loop(0, groups, sweep_one, 0)
+        return 0
+
+    lax.fori_loop(0, groups, sweep_one, 0, unroll=2)
     lax.fori_loop(0, half, send_dq, 0)
     lax.fori_loop(half, heads, merge_head, 0)
     lax.fori_loop(0, groups, sweep_two, 0)
@@ -504,7 +520,7 @@
             vmem((dim, wide), BF16),
             vmem((dim, wide), BF16),
             vmem((groups, group_keys, wide), BF16),
-            vmem((heads // 4, group_keys, 2 * rows), F32),
+            vmem((heads // 2, group_keys, 2 * rows), F32),
             vmem((group_keys, wide), BF16),
             vmem((group_keys, wide), BF16),
             vmem((dim, wide), F32),

time: 56.6 us -> 52.7 us (0.931)
  Pallas kernels: 55.8 us -> 51.8 us
    pallas_call x1, Pallas kernels: 53.7 us -> 49.8 us  [per_device(): pl.pallas_call(functools.partial(kernel, n_pb, n_ka), out_shape=(jax.Shap...]
where the time goes in v5:
time: 52.7 us; the launch traced here: 52.5 us
  Pallas kernels  51.8 us (98%)
  between operations  0.64 us (1%)
    pallas_call x1, Pallas kernels, per_device(): pl.pallas_call(functools.partial(kernel, n_pb, n_ka), out_shape=(jax.Shap...  49.8 us
    pallas_call x1, Pallas kernels, per_device(): pl.pallas_call(hand_over, out_shape=tuple((jax.ShapeDtypeStruct(one.shape...  2.07 us

profile of v5, /device:TPU:0, one launch (start us, length us, event | category | flops | bytes accessed | tf_op | source)
XLA Modules:
  0.0 52.5 jit_solution(154991312223640315)
XLA Ops:
  0.6 49.8 %shard_map.84 = (bf16[256,512]{1,0:T(8,128)(2,1)}, f32[256,512]{1,0:T(8,128)}, f32[128,128]{1,0:T(8,128)}, f32[128,128]{1,0:T(8,128)}) custom-call(s32[2,16]{1,0:T(2,128)} %mask_ref.1, bf16[256,1024]{1,0:T(8,128)(2,1)} %q_ref.1, bf16[128,128]{1,0:T(8,128)(2,1)} %k_ref.1, bf16[128,128]{1,0:T(8,128)(2,1)} %v_ref.1, bf16[256,1024]{1,0:T(8,128)(2,1)} %do_ref.1), custom_call_target="tpu_custom_call" | custom-call | flops 6442450944 | bytes 2097152 | tf_op jit(solution)/shard_map/pallas_call | solution.py:504
  50.4 2.1 %shard_map.85 = (bf16[256,512]{1,0:T(8,128)(2,1)}, f32[256,512]{1,0:T(8,128)}, f32[128,128]{1,0:T(8,128)}, f32[128,128]{1,0:T(8,128)}) custom-call(bf16[256,512]{1,0:T(8,128)(2,1)} %get-tuple-element.8.a, f32[256,512]{1,0:T(8,128)} %get-tuple-element.9.b, f32[128,128]{1,0:T(8,128)} %get-tuple-element.10.c, f32[128,128]{1,0:T(8,128)} %get-tuple-element.11.d), custom_call_target="tpu_custom_call" | custom-call | tf_op jit(solution)/shard_map/pallas_call | solution.py:572

commit v6 on v5

--- a/solution.py
+++ b/solution.py
@@ -161,7 +161,9 @@
         group = ring(z, k, groups)
         keys = group_rows(group, 0)
         k_turned[group] = keys.T
-        values_turned = group_rows(group, chunk).T
+        values_turned = jnp.concatenate(
+            [group_rows(group, chunk).T, jnp.ones((16, group_keys), BF16)], axis=0
+        )
         bias = [
             (mask_ref[0, group * group_blocks + b].astype(F32) - 1.0) * DEAD
             for b in range(group_blocks)
@@ -182,12 +184,10 @@
                 cols = head_columns(head_at(i), 2)
                 peak = functools.reduce(jnp.maximum, [p + one for p, one in zip(peaks, bias)])
                 low = []
-                total = jnp.zeros_like(peak)
                 for b in range(group_blocks):
                     shift = jnp.maximum(peak - bias[b], peaks[b])
                     part = wide_scores[(i - first) // 2, b * BLOCK : (b + 1) * BLOCK, :]
                     weight = jnp.exp2(part * log_scale - shift)
-                    total = total + jnp.sum(weight, axis=0, keepdims=True)
                     low.append(weight.astype(BF16))
                 low = jnp.concatenate(low, axis=0)
                 weights[group, :, cols] = low
@@ -196,8 +196,10 @@
                 new = jnp.maximum(old, peak)
                 keep, add = jnp.exp2(old - new), jnp.exp2(peak - new)
                 run_max[:, cols] = new
+                product = dot_nn(values_turned, low)
+                total = product[dim : dim + 1]
                 run_total[:, cols] = run_total[:, cols] * keep + total * add
-                out_acc[:, cols] = out_acc[:, cols] * keep + dot_nn(values_turned, low) * add
+                out_acc[:, cols] = out_acc[:, cols] * keep + product[0:dim] * add
                 peaks = later
 
         if middle is None:
@@ -224,27 +226,29 @@
 
         return 0
 
-    for k in range(1, min(3, groups)):
-        stage_z(k)
+    def first_middle():
+        stage_x(1)
+        if groups > 2:
+            stage_z(2)
+
     if groups > 1:
-        forward_group(0, lambda: stage_x(1))
+        stage_z(1)
+        forward_group(0, first_middle)
         stage_core(1)
         lax.fori_loop(1, groups, later_group, 0)
     else:
         forward_group(0)
 
-    def stat_copy(head, s):
+    def stat_copy(s):
         return remote(
-            stat_recv.at[panel, head], stat_recv.at[panel, head],
-            stat_send_sem.at[head, s], stat_recv_sem.at[panel, head],
-            {"ka": ring(panel, s, n_ka)},
-        )
-
-    def stat_arrived(head, source):
+            stat_recv.at[panel], stat_recv.at[panel],
+            stat_send_sem.at[s], stat_recv_sem.at[panel], {"ka": ring(panel, s, n_ka)},
+        )
+
+    def stat_arrived(source):
         remote(
-            stat_recv.at[source, head], stat_recv.at[source, head],
-            stat_send_sem.at[head, 0], stat_recv_sem.at[source, head],
-            {"ka": ring(panel, 1, n_ka)},
+            stat_recv.at[source], stat_recv.at[source],
+            stat_send_sem.at[0], stat_recv_sem.at[source], {"ka": ring(panel, 1, n_ka)},
         ).wait_recv()
 
     def part_copy(send, recv, send_sem, recv_sem, head):
@@ -260,16 +264,12 @@
             send_sem.at[0], recv_sem.at[source, local], {"ka": ring(panel, 1, n_ka)},
         ).wait_recv()
 
-    def finish_stats(i, _):
-        head = head_at(i)
-        cols = head_columns(head)
-        total = run_total[:, cols]
-        delta = jnp.sum(out_acc[:, cols] * do_turned[:, cols].astype(F32), axis=0, keepdims=True)
-        stat_recv[panel, head, 0:1, :] = run_max[:, cols] + jnp.log2(total)
-        stat_recv[panel, head, 1:2, :] = delta / total
-        for s in range(1, n_ka):
-            stat_copy(head, s).start()
-        return 0
+    totals = run_total[...]
+    deltas = jnp.sum(out_acc[...] * do_turned[...].astype(F32), axis=0, keepdims=True)
+    stat_recv[panel, 0:1, :] = run_max[...] + jnp.log2(totals)
+    stat_recv[panel, 1:2, :] = deltas / totals
+    for s in range(1, n_ka):
+        stat_copy(s).start()
 
     def finish_out(i, _):
         head = head_at(i)
@@ -287,25 +287,16 @@
 
         return 0
 
-    lax.fori_loop(0, heads, finish_stats, 0)
-    lax.fori_loop(0, heads, finish_out, 0)
-
-    def merge_head(i, _):
-        head = head_at(i)
-        cols = head_columns(head)
-        for s in range(1, n_ka):
-            stat_arrived(head, ring(panel, s, n_ka))
-        lses = [stat_recv[n, head, 0:1, :] for n in range(n_ka)]
-        peak = functools.reduce(jnp.maximum, lses)
-        lse = peak + jnp.log2(sum(jnp.exp2(one - peak) for one in lses))
-        row_lse[:, cols] = lse
-        row_delta[:, cols] = sum(
-            jnp.exp2(lses[n] - lse) * stat_recv[n, head, 1:2, :] for n in range(n_ka)
-        )
-        return 0
-
+    lax.fori_loop(0, heads, finish_out, 0, unroll=2)
+
+    for s in range(1, n_ka):
+        stat_arrived(ring(panel, s, n_ka))
+    lses = [stat_recv[n, 0:1, :] for n in range(n_ka)]
+    peak = functools.reduce(jnp.maximum, lses)
+    lse = peak + jnp.log2(sum(jnp.exp2(one - peak) for one in lses))
+    row_lse[...] = lse
+    row_delta[...] = sum(jnp.exp2(lses[n] - lse) * stat_recv[n, 1:2, :] for n in range(n_ka))
     half = heads // 2
-    lax.fori_loop(0, half, merge_head, 0)
 
     def back_group_of(k):
         return ring(z, k + 1, groups)
@@ -416,7 +407,6 @@
 
     lax.fori_loop(0, groups, sweep_one, 0, unroll=2)
     lax.fori_loop(0, half, send_dq, 0)
-    lax.fori_loop(half, heads, merge_head, 0)
     lax.fori_loop(0, groups, sweep_two, 0)
     lax.fori_loop(half, heads, send_dq, 0)
     last = groups - 1
@@ -431,11 +421,17 @@
             part_arrived(out_recv, out_send_sem, out_recv_sem, ring(panel, s, n_ka), local)
         lse = row_lse[:, cols]
         mixed = sum(
-            jnp.exp2(stat_recv[n, head, 0:1, :] - lse) * out_recv[n, local].astype(F32)
+            jnp.exp2(stat_recv[n, 0:1, cols] - lse) * out_recv[n, local].astype(F32)
             for n in range(n_ka)
         )
         att_ref[:, local * dim : (local + 1) * dim] = mixed.T.astype(BF16)
         dq_recv[panel, local] = (dq_acc[:, cols] * scale).astype(BF16)
+
+    for local in range(own_heads):
+        for s in range(1, n_ka):
+            part_arrived(dq_recv, dq_send_sem, dq_recv_sem, ring(panel, s, n_ka), local)
+        summed = sum(dq_recv[n, local].astype(F32) for n in range(n_ka))
+        qg_ref[:, local * dim : (local + 1) * dim] = summed.T
 
     total = x_total(last)
     for k in range(last):
@@ -444,12 +440,6 @@
     kg_ref[...] = total[0:chunk]
     vg_ref[...] = total[chunk : 2 * chunk]
 
-    for local in range(own_heads):
-        for s in range(1, n_ka):
-            part_arrived(dq_recv, dq_send_sem, dq_recv_sem, ring(panel, s, n_ka), local)
-        summed = sum(dq_recv[n, local].astype(F32) for n in range(n_ka))
-        qg_ref[:, local * dim : (local + 1) * dim] = summed.T
-
     def drain_group(k, _):
         x_copy(k).wait_send()
         core_copy(k, 0).wait_send()
@@ -468,9 +458,6 @@
 
     def drain_head(i, _):
         head = head_at(i)
-        for s in range(1, n_ka):
-            stat_copy(head, s).wait_send()
-
         @pl.when(foreign(head))
         def _():
             part_copy(out_send, out_recv, out_send_sem, out_recv_sem, head).wait_send()
@@ -479,6 +466,8 @@
         return 0
 
     lax.fori_loop(0, heads, drain_head, 0)
+    for s in range(1, n_ka):
+        stat_copy(s).wait_send()
 
 
 def hand_over(a, b, c, d, a_out, b_out, c_out, d_out, sem):
@@ -530,7 +519,7 @@
             vmem((groups, 1, wide), F32),
             vmem((1, wide), F32),
             vmem((1, wide), F32),
-            vmem((n_ka, heads, 8, rows), F32),
+            vmem((n_ka, 2, wide), F32),
             vmem((heads, dim, rows), BF16),
             vmem((n_ka, own_heads, dim, rows), BF16),
             vmem((heads, dim, rows), BF16),
@@ -547,8 +536,8 @@
             dma((groups,)),
             dma((groups,)),
             dma((2 * groups,)),
-            dma((heads, n_ka)),
-            dma((n_ka, heads)),
+            dma((n_ka,)),
+            dma((n_ka,)),
             dma((heads,)),
             dma((n_ka, own_heads)),
             dma((heads,)),

time: 52.7 us -> 51 us (0.968)
  Pallas kernels: 51.8 us -> 50.1 us
    pallas_call x1, Pallas kernels: 49.8 us -> 48 us  [per_device(): pl.pallas_call(functools.partial(kernel, n_pb, n_ka), out_shape=(jax.Shap...]
where the time goes in v6:
time: 51 us; the launch traced here: 50.8 us
  Pallas kernels  50.1 us (98%)
  between operations  0.64 us (1%)
    pallas_call x1, Pallas kernels, per_device(): pl.pallas_call(functools.partial(kernel, n_pb, n_ka), out_shape=(jax.Shap...  48 us
    pallas_call x1, Pallas kernels, per_device(): pl.pallas_call(hand_over, out_shape=tuple((jax.ShapeDtypeStruct(one.shape...  2.07 us

profile of v6, /device:TPU:0, one launch (start us, length us, event | category | flops | bytes accessed | tf_op | source)
XLA Modules:
  0.0 50.8 jit_solution(15541626491506850259)
XLA Ops:
  0.6 48.0 %shard_map.84 = (bf16[256,512]{1,0:T(8,128)(2,1)}, f32[256,512]{1,0:T(8,128)}, f32[128,128]{1,0:T(8,128)}, f32[128,128]{1,0:T(8,128)}) custom-call(s32[2,16]{1,0:T(2,128)} %mask_ref.1, bf16[256,1024]{1,0:T(8,128)(2,1)} %q_ref.1, bf16[128,128]{1,0:T(8,128)(2,1)} %k_ref.1, bf16[128,128]{1,0:T(8,128)(2,1)} %v_ref.1, bf16[256,1024]{1,0:T(8,128)(2,1)} %do_ref.1), custom_call_target="tpu_custom_call" | custom-call | flops 6442450944 | bytes 2097152 | tf_op jit(solution)/shard_map/pallas_call | solution.py:493
  48.7 2.1 %shard_map.85 = (bf16[256,512]{1,0:T(8,128)(2,1)}, f32[256,512]{1,0:T(8,128)}, f32[128,128]{1,0:T(8,128)}, f32[128,128]{1,0:T(8,128)}) custom-call(bf16[256,512]{1,0:T(8,128)(2,1)} %get-tuple-element.8.a, f32[256,512]{1,0:T(8,128)} %get-tuple-element.9.b, f32[128,128]{1,0:T(8,128)} %get-tuple-element.10.c, f32[128,128]{1,0:T(8,128)} %get-tuple-element.11.d), custom_call_target="tpu_custom_call" | custom-call | tf_op jit(solution)/shard_map/pallas_call | solution.py:561

commit v7 on v6

--- a/solution.py
+++ b/solution.py
@@ -187,8 +187,7 @@
                 for b in range(group_blocks):
                     shift = jnp.maximum(peak - bias[b], peaks[b])
                     part = wide_scores[(i - first) // 2, b * BLOCK : (b + 1) * BLOCK, :]
-                    weight = jnp.exp2(part * log_scale - shift)
-                    low.append(weight.astype(BF16))
+                    low.append(jnp.exp2((part * log_scale - shift).astype(BF16)))
                 low = jnp.concatenate(low, axis=0)
                 weights[group, :, cols] = low
                 group_max[group, :, cols] = peak
@@ -470,13 +469,18 @@
         stat_copy(s).wait_send()
 
 
-def hand_over(a, b, c, d, a_out, b_out, c_out, d_out, sem):
-    pairs = ((a, a_out), (b, b_out), (c, c_out), (d, d_out))
-    copies = [pltpu.make_async_copy(src, dst, sem.at[i]) for i, (src, dst) in enumerate(pairs)]
-    for copy in copies:
-        copy.start()
-    for copy in copies:
-        copy.wait()
+def hand_over(*refs):
+    sources, targets, stops, read_sem, write_sem = refs[:4], refs[4:8], refs[8:12], refs[12], refs[13]
+    order = (2, 3, 0, 1)
+    reads = [pltpu.make_async_copy(sources[i], stops[i], read_sem.at[i]) for i in range(4)]
+    writes = [pltpu.make_async_copy(stops[i], targets[i], write_sem.at[i]) for i in range(4)]
+    for i in order:
+        reads[i].start()
+    for i in order:
+        reads[i].wait()
+        writes[i].start()
+    for i in order:
+        writes[i].wait()
 
 
 def per_device(n_pb, n_ka, queries, keys, values, dout, block_mask):
@@ -562,8 +566,8 @@
         hand_over,
         out_shape=tuple(jax.ShapeDtypeStruct(one.shape, one.dtype) for one in results),
         in_specs=[pl.BlockSpec(memory_space=pl.ANY)] * 4,
-        out_specs=[pl.BlockSpec(memory_space=pltpu.VMEM)] * 4,
-        scratch_shapes=[dma((4,))],
+        out_specs=[pl.BlockSpec(memory_space=pl.ANY)] * 4,
+        scratch_shapes=[vmem(one.shape, one.dtype) for one in results] + [dma((4,))] * 2,
         compiler_params=pltpu.CompilerParams(vmem_limit_bytes=63 * 2**20),
     )(*results)
 

time: 51 us -> 50.9 us (level)
  no operation moved by 1% of the time
where the time goes in v7:
time: 50.9 us; the launch traced here: 50.7 us
  Pallas kernels  50.1 us (98%)
  between operations  0.64 us (1%)
    pallas_call x1, Pallas kernels, per_device(): pl.pallas_call(functools.partial(kernel, n_pb, n_ka), out_shape=(jax.Shap...  48 us
    pallas_call x1, Pallas kernels, per_device(): pl.pallas_call(hand_over, out_shape=tuple((jax.ShapeDtypeStruct(one.shape...  2.06 us

profile of v7, /device:TPU:0, one launch (start us, length us, event | category | flops | bytes accessed | tf_op | source)
XLA Modules:
  0.0 50.7 jit_solution(3631289462034847722)
XLA Ops:
  0.6 48.0 %shard_map.84 = (bf16[256,512]{1,0:T(8,128)(2,1)}, f32[256,512]{1,0:T(8,128)}, f32[128,128]{1,0:T(8,128)}, f32[128,128]{1,0:T(8,128)}) custom-call(s32[2,16]{1,0:T(2,128)} %mask_ref.1, bf16[256,1024]{1,0:T(8,128)(2,1)} %q_ref.1, bf16[128,128]{1,0:T(8,128)(2,1)} %k_ref.1, bf16[128,128]{1,0:T(8,128)(2,1)} %v_ref.1, bf16[256,1024]{1,0:T(8,128)(2,1)} %do_ref.1), custom_call_target="tpu_custom_call" | custom-call | flops 6442450944 | bytes 2097152 | tf_op jit(solution)/shard_map/pallas_call | solution.py:497
  48.7 2.1 %shard_map.85 = (bf16[256,512]{1,0:T(8,128)(2,1)}, f32[256,512]{1,0:T(8,128)}, f32[128,128]{1,0:T(8,128)}, f32[128,128]{1,0:T(8,128)}) custom-call(bf16[256,512]{1,0:T(8,128)(2,1)} %get-tuple-element.8.refs_0_, f32[256,512]{1,0:T(8,128)} %get-tuple-element.9.refs_1_, f32[128,128]{1,0:T(8,128)} %get-tuple-element.10.refs_2_, f32[128,128]{1,0:T(8,128)} %get-tuple-element.11.refs_3_), custom_call_target="tpu_custom_call" | custom-call | tf_op jit(solution)/shard_map/pallas_call | solution.py:565

commit v8 on v7

--- a/solution.py
+++ b/solution.py
@@ -187,7 +187,7 @@
                 for b in range(group_blocks):
                     shift = jnp.maximum(peak - bias[b], peaks[b])
                     part = wide_scores[(i - first) // 2, b * BLOCK : (b + 1) * BLOCK, :]
-                    low.append(jnp.exp2((part * log_scale - shift).astype(BF16)))
+                    low.append(jnp.exp2(part * log_scale - shift).astype(BF16))
                 low = jnp.concatenate(low, axis=0)
                 weights[group, :, cols] = low
                 group_max[group, :, cols] = peak
@@ -404,7 +404,7 @@
         send_core(k)
         return 0
 
-    lax.fori_loop(0, groups, sweep_one, 0, unroll=2)
+    lax.fori_loop(0, groups, sweep_one, 0, unroll=4 if groups % 4 == 0 else 1)
     lax.fori_loop(0, half, send_dq, 0)
     lax.fori_loop(0, groups, sweep_two, 0)
     lax.fori_loop(half, heads, send_dq, 0)

time: 50.9 us -> 50.8 us (level)
  no operation moved by 1% of the time
where the time goes in v8:
time: 50.8 us; the launch traced here: 50.6 us
  Pallas kernels  50 us (98%)
  between operations  0.64 us (1%)
    pallas_call x1, Pallas kernels, per_device(): pl.pallas_call(functools.partial(kernel, n_pb, n_ka), out_shape=(jax.Shap...  47.9 us
    pallas_call x1, Pallas kernels, per_device(): pl.pallas_call(hand_over, out_shape=tuple((jax.ShapeDtypeStruct(one.shape...  2.06 us

profile of v8, /device:TPU:0, one launch (start us, length us, event | category | flops | bytes accessed | tf_op | source)
XLA Modules:
  0.0 50.6 jit_solution(6710226592347362962)
XLA Ops:
  0.6 47.9 %shard_map.84 = (bf16[256,512]{1,0:T(8,128)(2,1)}, f32[256,512]{1,0:T(8,128)}, f32[128,128]{1,0:T(8,128)}, f32[128,128]{1,0:T(8,128)}) custom-call(s32[2,16]{1,0:T(2,128)} %mask_ref.1, bf16[256,1024]{1,0:T(8,128)(2,1)} %q_ref.1, bf16[128,128]{1,0:T(8,128)(2,1)} %k_ref.1, bf16[128,128]{1,0:T(8,128)(2,1)} %v_ref.1, bf16[256,1024]{1,0:T(8,128)(2,1)} %do_ref.1), custom_call_target="tpu_custom_call" | custom-call | flops 6442450944 | bytes 2097152 | tf_op jit(solution)/shard_map/pallas_call | solution.py:497
  48.6 2.1 %shard_map.85 = (bf16[256,512]{1,0:T(8,128)(2,1)}, f32[256,512]{1,0:T(8,128)}, f32[128,128]{1,0:T(8,128)}, f32[128,128]{1,0:T(8,128)}) custom-call(bf16[256,512]{1,0:T(8,128)(2,1)} %get-tuple-element.8.refs_0_, f32[256,512]{1,0:T(8,128)} %get-tuple-element.9.refs_1_, f32[128,128]{1,0:T(8,128)} %get-tuple-element.10.refs_2_, f32[128,128]{1,0:T(8,128)} %get-tuple-element.11.refs_3_), custom_call_target="tpu_custom_call" | custom-call | tf_op jit(solution)/shard_map/pallas_call | solution.py:565
